TPU v7x, 32 devices: a whole 2x2x4 slice. The times are simulated.
32 devices in a mesh: gx: 4 (over y, x), gy: 4 (over z), gz: 2 (over core).
Axes of the slice: x: 2, y: 2, z: 4, core: 2. Of those that a mesh axis runs over, the one named last changes fastest.
Arguments:
- positions: float32 [3, 1024], P(None, ('gx', 'gy', 'gz')), may hold values from 0 to 35.2, as said below
- species: int32 [1024], P(('gx', 'gy', 'gz')), may hold values from 0 to 63
- neighbours: int32 [32, 1024], P(None, ('gx', 'gy', 'gz')), may hold values from 0 to 863, as said below
- embed_center: float32 [64, 1024], replicated, may hold values from -3.5 to 3.5
- embed_neigh: float32 [64, 1024], replicated, may hold values from -3.5 to 3.5
- embed_radial: float32 [8, 1024], replicated, may hold values from -3.5 to 3.5
- value_proj: float32 [1024, 64], replicated, may hold values from -0.1875 to 0.1875
- env_weight: float32 [2, 1024, 64], replicated, may hold values from -0.1875 to 0.1875
- latent_weight: float32 [2, 1216, 1024], replicated, may hold values from -0.15625 to 0.15625
- path_weight: float32 [9, 64], replicated, may hold values from -4 to 4
- out_weight: float32 [1024], replicated, may hold values from -0.1875 to 0.1875
- scale_table: float32 [64], replicated, may hold values from 0.2 to 1
- shift_table: float32 [64], replicated, may hold values from -4 to 4
- cotangent: float32 [1024], P(('gx', 'gy', 'gz')), may hold values from -6 to 6
Outputs:
- atom_energy: float32 [1024], P(('gx', 'gy', 'gz'))
- position_grad: float32 [3, 1024], P(None, ('gx', 'gy', 'gz'))
- grad_embed_center: float32 [64, 1024], replicated
- grad_embed_neigh: float32 [64, 1024], replicated
- grad_embed_radial: float32 [8, 1024], replicated
- grad_value_proj: float32 [1024, 64], replicated
- grad_env_weight: float32 [2, 1024, 64], replicated
- grad_latent_weight: float32 [2, 1216, 1024], replicated
- grad_path_weight: float32 [9, 64], replicated
- grad_out_weight: float32 [1024], replicated
- grad_scale_table: float32 [64], replicated
- grad_shift_table: float32 [64], replicated
Inputs may be any that keep to these rules, and one draw needn't show every extreme that they name: Column i = d * 32 + a lists atom i's neighbours as slots (bx * 9 + by * 3 + bz) * 32 + a' of a table of the atoms of the 27 devices at grid offsets (bx - 1, by - 1, bz - 1) around d; the real neighbours come first, lie on devices that exist, are distinct and are closer than 5 to atom i; the other slots hold 416 + a; at most 32 real neighbours per atom. `positions`: atoms of device d lie in its own box of the grid of devices, at distances 1.5 or more from each other.
All inputs are finite; a program needn't handle non-finite values.
Results may differ from a plain program's by a relative error of at most 0.0003.
Values sent between devices are 32-bit elements; how exact they have to be, the bound alone decides.
No kernel may reach another device: no remote copies, remote signals or barrier semaphores. Data moves between devices by JAX's collectives and lax.ppermute only.
A program may use at most 256 MiB of HBM per device.

v0:
```python
import math

import jax
import jax.numpy as jnp
import numpy as np
from jax import lax
from jax.sharding import PartitionSpec as P

CHANNELS = 64
NSPEC = 64
NBESSEL = 8
NB = 32


CUTOFF = 5.0
ROOT_HALF = 0.7071067811865476
HALF_ROOT = 0.7071067811865476
SIXTH_ROOT = 0.4082482904638631
PRECISE = lax.Precision.HIGHEST
BASIS = np.array(
    [
        [[HALF_ROOT, 0.0, 0.0], [0.0, -HALF_ROOT, 0.0], [0.0, 0.0, 0.0]],
        [[SIXTH_ROOT, 0.0, 0.0], [0.0, SIXTH_ROOT, 0.0], [0.0, 0.0, -2.0 * SIXTH_ROOT]],
        [[0.0, HALF_ROOT, 0.0], [HALF_ROOT, 0.0, 0.0], [0.0, 0.0, 0.0]],
        [[0.0, 0.0, HALF_ROOT], [0.0, 0.0, 0.0], [HALF_ROOT, 0.0, 0.0]],
        [[0.0, 0.0, 0.0], [0.0, 0.0, HALF_ROOT], [0.0, HALF_ROOT, 0.0]],
    ]
)


def shifted(value, axis, by):
    length = lax.axis_size(axis)
    pairs = [(i, i + by) for i in range(length) if 0 <= i + by < length]
    return lax.ppermute(value, axis, pairs)


def with_halo(cells, sides, width):
    for axis, dim in sides:
        count = lax.axis_size(axis)
        ends = count - 1
        head = lax.slice_in_dim(cells, 0, width, axis=dim)
        tail = lax.slice_in_dim(cells, cells.shape[dim] - width, cells.shape[dim], axis=dim)
        cells = jnp.concatenate(
            [
                lax.ppermute(tail, axis, [(i, (i + 1) % count) for i in range(ends)]),
                cells,
                lax.ppermute(head, axis, [((i + 1) % count, i) for i in range(ends)]),
            ],
            axis=dim,
        )
    return cells


def product(left_side, right_side):
    return jnp.dot(left_side, right_side, precision=PRECISE, preferred_element_type=jnp.float32)


def geometry(centre, neighbour, live_mask):
    padding = jnp.array([2.5, 0.0, 0.0], jnp.float32)[:, None]
    displacement = (neighbour - centre) * live_mask[None] + (1.0 - live_mask)[None] * padding
    distance = jnp.sqrt(jnp.sum(displacement * displacement, axis=0))
    scaled = distance / CUTOFF
    sixth_power = scaled**6
    smooth = live_mask * (
        1.0
        - 28.0 * sixth_power
        + 48.0 * sixth_power * scaled
        - 21.0 * sixth_power * scaled * scaled
    )
    orders = (jnp.arange(NBESSEL) + 1).astype(jnp.float32)[:, None]
    radial = (
        smooth[None]
        * math.sqrt(2.0 / CUTOFF)
        * jnp.sin(orders * (math.pi / CUTOFF) * distance[None])
        / distance[None]
    )
    direction = displacement / distance[None]
    harmonic_basis = jnp.asarray(BASIS, jnp.float32)
    second = math.sqrt(7.5) * jnp.einsum(
        "mik,in,kn->mn", harmonic_basis, direction, direction, precision=PRECISE
    )
    harmonics = jnp.concatenate(
        [jnp.ones_like(distance)[None], math.sqrt(3.0) * direction, second], 0
    )
    return (smooth, radial, harmonics)


def embedding(
    radial, smooth, centre_species, neighbour_species, embed_center, embed_neigh, embed_radial
):
    species_ids = jnp.arange(NSPEC, dtype=jnp.int32)[None]
    centre_hot = (centre_species[:, None] == species_ids).astype(jnp.float32)
    neighbour_hot = (neighbour_species[:, None] == species_ids).astype(jnp.float32)
    before = (
        product(centre_hot, embed_center)
        + product(neighbour_hot, embed_neigh)
        + product(radial.T, embed_radial)
    )
    return jax.nn.silu(before) * smooth[:, None]


def environment(latent, harmonics, env_weight):
    weights = product(latent, env_weight).T
    edge_count = weights.shape[1]
    atom_count = edge_count // NB
    summed = jnp.sum(
        (harmonics[:, None, :] * weights[None]).reshape(9, CHANNELS, NB, atom_count), axis=2
    ) * NB ** (-0.5)
    return jnp.broadcast_to(summed[:, :, None, :], (9, CHANNELS, NB, atom_count)).reshape(
        9, CHANNELS, edge_count
    )


def invariants(features, surround):
    parts = jnp.concatenate(
        [
            features[0:1] * surround[0:1],
            jnp.sum(features[1:4] * surround[1:4], 0, keepdims=True),
            jnp.sum(features[4:9] * surround[4:9], 0, keepdims=True),
        ],
        0,
    )
    return parts.reshape(3 * CHANNELS, -1).T


def update(latent, features, surround, smooth, latent_weight):
    joined = jnp.concatenate([latent, invariants(features, surround)], 1)
    return (latent + smooth[:, None] * jax.nn.silu(product(joined, latent_weight))) * ROOT_HALF


def couple(features, surround, path_weight):
    harmonic_basis = jnp.asarray(BASIS, jnp.float32)
    scalar_part, vector_part, tensor_part = (features[0], features[1:4], features[4:9])
    env_scalar, env_vector, env_tensor = (surround[0], surround[1:4], surround[4:9])
    path_gain = path_weight[:, :, None]
    crossed = jnp.stack(
        [
            vector_part[1] * env_vector[2] - vector_part[2] * env_vector[1],
            vector_part[2] * env_vector[0] - vector_part[0] * env_vector[2],
            vector_part[0] * env_vector[1] - vector_part[1] * env_vector[0],
        ]
    )
    turned = jnp.einsum(
        "mik,mcn,kcn->icn", harmonic_basis, tensor_part, env_vector, precision=PRECISE
    )
    paired = jnp.einsum(
        "mik,icn,kcn->mcn", harmonic_basis, vector_part, env_vector, precision=PRECISE
    )
    new_scalar = path_gain[0] * scalar_part * env_scalar + path_gain[1] * jnp.sum(
        vector_part * env_vector, 0
    )
    new_vector = (
        path_gain[2] * scalar_part[None] * env_vector
        + path_gain[3] * vector_part * env_scalar[None]
        + path_gain[4] * crossed
        + path_gain[5] * turned
    )
    new_tensor = (
        path_gain[6] * paired
        + path_gain[7] * scalar_part[None] * env_tensor
        + path_gain[8] * tensor_part * env_scalar[None]
    )
    return jnp.concatenate([new_scalar[None], new_vector, new_tensor], 0)


def readout(latent, smooth, species, out_weight, scale_table, shift_table):
    edge_energy = product(latent, out_weight[:, None])[:, 0] * smooth
    atom_count = species.shape[0]
    summed = jnp.sum(edge_energy.reshape(NB, atom_count), 0)
    species_hot = (jnp.arange(NSPEC, dtype=jnp.int32)[:, None] == species[None]).astype(jnp.float32)
    return (
        product(scale_table[None], species_hot)[0] * summed
        + product(shift_table[None], species_hot)[0]
    )


def fold_along_x(ghost_grad):
    return (
        ghost_grad[:, 1:2]
        + shifted(ghost_grad[:, 2:3], "gx", 1)
        + shifted(ghost_grad[:, 0:1], "gx", -1)
    )


def fold_along_y(ghost_grad):
    return (
        ghost_grad[:, :, 1:2]
        + shifted(ghost_grad[:, :, 2:3], "gy", 1)
        + shifted(ghost_grad[:, :, 0:1], "gy", -1)
    )


def fold_along_z(ghost_grad):
    return (
        ghost_grad[:, :, :, 1:2]
        + shifted(ghost_grad[:, :, :, 2:3], "gz", 1)
        + shifted(ghost_grad[:, :, :, 0:1], "gz", -1)
    )


def per_device(
    positions,
    species,
    neighbours,
    embed_center,
    embed_neigh,
    embed_radial,
    value_proj,
    env_weight,
    latent_weight,
    path_weight,
    out_weight,
    scale_table,
    shift_table,
    cotangent,
):
    atom_count = positions.shape[1]
    carried = jnp.concatenate([positions, species.astype(jnp.float32)[None]], 0).reshape(
        4, 1, 1, 1, atom_count
    )
    ghost_table = with_halo(carried, (("gx", 1), ("gy", 2), ("gz", 3)), 1)
    ghost_table = ghost_table.reshape(4, 27 * atom_count)
    slot_table = neighbours.reshape(-1)
    own_slot = 13 * atom_count + jnp.arange(atom_count, dtype=jnp.int32)
    live_mask = (neighbours != own_slot[None]).astype(jnp.float32).reshape(-1)
    neighbour_species = ghost_table[3].astype(jnp.int32)[slot_table]
    centre_species = jnp.tile(species, NB)

    def first_section(ghost_pos, embed_center, embed_neigh, embed_radial, value_proj):
        centre = jnp.tile(ghost_pos[:, 13 * atom_count : 14 * atom_count], (1, NB))
        smooth, radial, harmonics = geometry(centre, ghost_pos[:, slot_table], live_mask)
        latent = embedding(
            radial,
            smooth,
            centre_species,
            neighbour_species,
            embed_center,
            embed_neigh,
            embed_radial,
        )
        features = harmonics[:, None, :] * product(latent, value_proj).T[None]
        return (latent, features, smooth, harmonics)

    def first_layer(latent, features, smooth, harmonics, layer_env, layer_latent, path_weight):
        surround = environment(latent, harmonics, layer_env)
        return (
            update(latent, features, surround, smooth, layer_latent),
            couple(features, surround, path_weight),
        )

    def second_layer(latent, features, smooth, harmonics, layer_env, layer_latent):
        surround = environment(latent, harmonics, layer_env)
        return update(latent, features, surround, smooth, layer_latent)

    def final_section(latent, smooth, out_weight, scale_table, shift_table):
        return readout(latent, smooth, species, out_weight, scale_table, shift_table)

    (latent0, field0, smooth, harmonics), pull_embed = jax.vjp(
        first_section, ghost_table[0:3], embed_center, embed_neigh, embed_radial, value_proj
    )
    (latent1, field1), pull_first = jax.vjp(
        first_layer,
        latent0,
        field0,
        smooth,
        harmonics,
        env_weight[0],
        latent_weight[0],
        path_weight,
    )
    latent2, pull_second = jax.vjp(
        second_layer, latent1, field1, smooth, harmonics, env_weight[1], latent_weight[1]
    )
    energy, pull_out = jax.vjp(final_section, latent2, smooth, out_weight, scale_table, shift_table)
    d_latent2, d_smooth_out, d_out, d_scale, d_shift = pull_out(cotangent)
    d_latent1, d_field1, d_smooth_late, d_harm_late, d_env_late, d_lat_late = pull_second(d_latent2)
    d_env_late, d_lat_late, d_out, d_scale, d_shift = lax.psum(
        (d_env_late, d_lat_late, d_out, d_scale, d_shift), ("gx", "gy", "gz")
    )
    d_latent0, d_field0, d_smooth_early, d_harm_early, d_env_early, d_lat_early, d_path = (
        pull_first((d_latent1, d_field1))
    )
    d_ghost, d_center, d_neigh, d_radial, d_value = pull_embed(
        (
            d_latent0,
            d_field0,
            d_smooth_out + d_smooth_late + d_smooth_early,
            d_harm_late + d_harm_early,
        )
    )
    d_env_early, d_lat_early, d_path, d_center, d_neigh, d_radial, d_value = lax.psum(
        (d_env_early, d_lat_early, d_path, d_center, d_neigh, d_radial, d_value), ("gx", "gy", "gz")
    )
    ghost_grad = d_ghost.reshape(3, 3, 3, 3, atom_count)
    ghost_grad = fold_along_x(fold_along_y(fold_along_z(ghost_grad)))
    position_grad = ghost_grad.reshape(3, atom_count)
    return (
        energy,
        position_grad,
        d_center,
        d_neigh,
        d_radial,
        d_value,
        jnp.stack([d_env_early, d_env_late]),
        jnp.stack([d_lat_early, d_lat_late]),
        d_path,
        d_out,
        d_scale,
        d_shift,
    )


def solution(mesh):
    return jax.shard_map(
        per_device,
        mesh=mesh,
        in_specs=(
            P(None, ("gx", "gy", "gz")),
            P(("gx", "gy", "gz")),
            P(None, ("gx", "gy", "gz")),
            P(),
            P(),
            P(),
            P(),
            P(),
            P(),
            P(),
            P(),
            P(),
            P(),
            P(("gx", "gy", "gz")),
        ),
        out_specs=(
            P(("gx", "gy", "gz")),
            P(None, ("gx", "gy", "gz")),
            P(),
            P(),
            P(),
            P(),
            P(),
            P(),
            P(),
            P(),
            P(),
            P(),
        ),
        check_vma=False,
    )
```

profile of v0, /device:TPU:0, one launch (start us, length us, event | category | flops | bytes accessed | tf_op | source)
XLA Modules:
  0.0 648.6 jit_solution(12652008840353717234)
XLA Ops:
  9.9 5.5 collective-permute-start
  19.3 4.9 fusion.69
  25.7 4.6 collective-permute-start.2
  33.0 3.0 collective-permute-start.4
  37.3 3.0 gather_fusion.1
  40.3 4.5 gather_fusion
  49.7 6.1 broadcast_multiply_fusion
  55.8 2.1 copy-done.1
  57.9 2.8 convolution_bitcast_fusion.5
  63.6 5.6 convolution_bitcast_fusion.6
  75.9 2.7 broadcast_in_dim.63
  78.6 3.0 copy.276
  81.6 2.8 slice_bitcast_fusion
  85.5 21.5 %add_multiply_fusion.1 = (f32[1024,1024]{0,1:T(8,128)S(1)}, f32[1024,1024]{0,1:T(8,128)}) fusion(f32[1024,1024]{0,1:T(8,128)S(1)} %copy-done.2, f32[1024]{0:T(1024)S(1)} %copy-done.112, f32[2,1216,1024]{2,1,0:T(8,128)} %param.25, f32[1024,192]{0,1:T(8,128)S(1)} %bitcast.379), kind=kOutput, calls=%fused_computation.56 | convolution fusion | flops 15309406208 | bytes 22548480 | tf_op jit(solution)/shard_map/jvp()/dot_general | solution.py:55
  107.0 2.0 copy-done.12
  109.0 3.5 convolution_bitcast_fusion.4
  131.1 2.7 copy.288
  133.7 3.5 copy.289
  138.7 1.9 copy.279
  140.7 2.1 broadcast_in_dim.73
  142.8 2.7 copy.292
  145.7 7.7 %fusion.44 = f32[3,64,1024]{2,0,1:T(4,128)S(1)} fusion(f32[5,3,3,1]{0,1,2,3:T(4,128)} %constant.138, f32[64,1024,5]{1,2,0:T(8,128)} %copy.289, f32[64,1024,3]{1,2,0:T(4,128)} %copy.288), kind=kOutput, calls=%fused_computation.81 | convolution fusion | flops 36372480 | bytes 2883764 | tf_op jit(solution)/shard_map/jvp(mik,mcn,kcn->icn)/dot_general | solution.py:143
  154.6 2.5 multiply_reduce_fusion.25
  160.5 3.2 copy.298
  163.7 6.9 %fusion.39 = f32[5,64,1024]{2,0,1:T(8,128)S(1)} fusion(f32[5,3,3,1]{0,2,1,3:T(4,128)} %constant.139, f32[64,1024,3]{1,2,0:T(4,128)} %copy.294, f32[64,1024,3]{1,2,0:T(4,128)} %copy.288), kind=kOutput, calls=%fused_computation.78 | convolution fusion | flops 35979264 | bytes 2883764 | tf_op jit(solution)/shard_map/jvp(mik,icn,kcn->mcn)/dot_general | solution.py:146
  170.7 2.4 multiply_reduce_fusion.18
  174.2 20.8 %fusion.20 = (f32[1024]{0:T(1024)}, f32[1024,1024]{0,1:T(8,128)S(1)}) fusion(f32[1024]{0:T(1024)S(1)} %copy-done.173, f32[1024]{0:T(1024)S(1)} %copy-done.157, f32[2,1216,1024]{2,1,0:T(8,128)} %param.25, f32[1024,192]{0,1:T(8,128)S(1)} %bitcast.381, f32[1024,1024]{0,1:T(8,128)S(1)} %copy-done.13), kind=kOutput, calls=%fused_computation.41 | convolution fusion | flops 15310453760 | bytes 14168064 | tf_op jit(solution)/shard_map/jvp()/dot_general | solution.py:55
  195.0 21.0 %convolution_bitcast_fusion = f32[1,1216,1024]{2,1,0:T(8,128)} fusion(f32[1024,192]{0,1:T(8,128)S(1)} %bitcast.382, f32[1024,1024]{0,1:T(8,128)S(1)} %copy-done.13, f32[1024,1024]{0,1:T(8,128)S(1)} %get-tuple-element.167, f32[1024]{0:T(1024)S(1)} %copy-done.155, f32[1024]{0:T(1024)S(1)} %copy-done.173, f32[1024]{0:T(1024)S(1)} %copy-done.157), kind=kOutput, calls=%fused_computation.38 | convolution fusion | flops 15313600512 | bytes 14168064 | tf_op jit(solution)/shard_map/transpose(jvp())/dot_general | solution.py:55
  216.0 21.2 %fusion.7 = f32[1024,1216]{0,1:T(8,128)} fusion(f32[2,1216,1024]{2,1,0:T(8,128)S(1)} %bitcast.407, f32[1024,1024]{0,1:T(8,128)S(1)} %get-tuple-element.167, f32[1024]{0:T(1024)S(1)} %copy-done.155, f32[1024]{0:T(1024)S(1)} %copy-done.173, f32[1024]{0:T(1024)S(1)} %copy-done.157), kind=kOutput, calls=%fused_computation.20 | convolution fusion | flops 15312355328 | bytes 14168064 | tf_op jit(solution)/shard_map/transpose(jvp())/dot_general | solution.py:55
  237.3 1.9 copy.303
  250.7 5.1 copy.300
  255.8 3.6 reduce_sum.358
  260.5 3.5 multiply_reduce_fusion.5
  264.0 7.1 %convolution_bitcast_fusion.2 = f32[1,1024,64]{1,2,0:T(8,128)} fusion(f32[1024,1024]{0,1:T(8,128)} %copy-done.12, f32[64,1024]{0,1:T(8,128)S(1)} %bitcast.371), kind=kOutput, calls=%fused_computation.94 | convolution fusion | flops 805306368 | bytes 4718592 | tf_op jit(solution)/shard_map/transpose(jvp())/dot_general | solution.py:55
  271.2 7.6 %multiply_reduce_fusion.9 = (f32[1024]{0:T(1024)}, f32[1024,1024]{0,1:T(8,128)S(1)}) fusion(f32[1024,1024]{0,1:T(8,128)S(1)} %copy-done.183, f32[64,1024]{0,1:T(8,128)S(1)} %bitcast.372, f32[2,1024,64]{1,2,0:T(8,128)S(1)} %copy-done.67, f32[1024,1216]{0,1:T(8,128)} %fusion.7, f32[1024]{0:T(1024)S(1)} %copy-done.174, f32[1024]{0:T(1024)S(1)} %copy-done.158), kind=kOutput, calls=%fused_computation.52 | convolution fusion | flops 816839680 | bytes 13381632 | tf_op jit(solution)/shard_map/transpose(jvp())/dot_general | solution.py:55
  278.8 20.8 %convolution_bitcast_fusion.1 = f32[1,1216,1024]{2,1,0:T(8,128)} fusion(f32[1024,192]{0,1:T(8,128)S(1)} %bitcast.380, f32[1024,1024]{0,1:T(8,128)S(1)} %copy-done.3, f32[1024,1024]{0,1:T(8,128)S(1)} %copy-done.183, f32[1024,1024]{0,1:T(8,128)S(1)} %get-tuple-element.165, f32[1024]{0:T(1024)S(1)} %copy-done.156), kind=kOutput, calls=%fused_computation.39 | convolution fusion | flops 15312551936 | bytes 18354176 | tf_op jit(solution)/shard_map/transpose(jvp())/dot_general | solution.py:55
  299.8 18.0 %fusion.11 = f32[1024,1216]{0,1:T(8,128)S(1)} fusion(f32[2,1216,1024]{2,1,0:T(8,128)S(1)} %bitcast.409, f32[1024,1024]{0,1:T(8,128)S(1)} %copy-done.183, f32[1024,1024]{0,1:T(8,128)S(1)} %get-tuple-element.165, f32[1024]{0:T(1024)S(1)} %copy-done.156), kind=kOutput, calls=%fused_computation.24 | convolution fusion | flops 15311306752 | bytes 18354176 | tf_op jit(solution)/shard_map/transpose(jvp())/dot_general | solution.py:55
  320.6 8.5 %multiply_reduce_fusion = (f32[64,1024,5]{1,2,0:T(8,128)S(1)}, f32[64,1024,5,3]{1,2,3,0:T(8,128)S(1)}) fusion(f32[64,1024,3]{1,2,0:T(4,128)S(1)} %copy-done.6, f32[5,3,3,1]{0,1,2,3:T(4,128)S(1)} %copy-done.129, f32[3,64,1024,1]{2,1,0,3:T(8,128)S(1)} %copy-done.35), kind=kOutput, calls=%fused_computation.6 | convolution fusion | flops 37027840 | bytes 6815924 | tf_op jit(solution)/shard_map/transpose(jvp(mik,mcn,kcn->icn))/dot_general | solution.py:143
  329.1 4.7 multiply_reduce_fusion.1
  333.9 4.6 slice_multiply_fusion.1
  338.4 7.9 %multiply_reduce_fusion.10 = (f32[64,1024,3]{1,2,0:T(4,128)S(1)}, f32[64,1024,3,3]{1,3,2,0:T(4,128)S(1)}) fusion(f32[64,1024,3]{1,2,0:T(4,128)S(1)} %copy-done.6, f32[5,3,3,1]{0,2,1,3:T(4,128)S(1)} %copy-done.128, f32[5,64,1024,1]{2,1,0,3:T(8,128)S(1)} %get-tuple-element.81), kind=kOutput, calls=%fused_computation.64 | convolution fusion | flops 36372480 | bytes 5243060 | tf_op jit(solution)/shard_map/transpose(jvp(mik,icn,kcn->mcn))/dot_general | solution.py:146
  348.8 3.4 multiply_reduce_fusion.22
  352.2 2.6 fusion.77
  356.5 3.5 copy.307
  360.0 3.0 reduce_sum.371
  363.1 3.1 multiply_reduce_fusion.3
  366.2 7.3 %convolution_bitcast_fusion.3 = f32[1,1024,64]{1,2,0:T(8,128)} fusion(f32[1024,1024]{0,1:T(8,128)} %copy-done.1, f32[64,1024]{0,1:T(8,128)S(1)} %bitcast.359), kind=kOutput, calls=%fused_computation.95 | convolution fusion | flops 805306368 | bytes 4718592 | tf_op jit(solution)/shard_map/transpose(jvp())/dot_general | solution.py:55
  373.5 3.5 fusion.87
  377.9 4.9 fusion.172
  382.8 9.4 %multiply_reduce_fusion.8 = (f32[1024]{0:T(1024)S(1)}, f32[1024,1024]{0,1:T(8,128)S(1)}) fusion(f32[1024,1024]{0,1:T(8,128)S(1)} %copy-done.181, f32[1024]{0:T(1024)S(1)} %copy-done.113, f32[64,1024]{1,0:T(8,128)S(1)} %get-tuple-element.17, f32[1024,64]{0,1:T(8,128)S(1)} %copy-done, f32[1024,1024]{0,1:T(8,128)S(1)} %fusion.87, ...), kind=kOutput, calls=%fused_computation.51 | convolution fusion | flops 823131136 | bytes 21504000 | tf_op jit(solution)/shard_map/transpose(jvp())/dot_general | solution.py:55
  392.2 3.1 fusion.72
  395.3 3.1 fusion.70
  400.0 4.7 fusion.104
  404.8 5.9 fusion.48
  411.5 6.4 scatter_fusion
  419.7 3.0 collective-permute-start.6
  423.4 5.8 fusion.114
  429.4 6.7 %fusion.47 = f32[1,1024]{1,0:T(1,128)S(1)} fusion(f32[1024,1]{0,1:T(1,128)S(1)} %bitcast.395, f32[1024,1024]{0,1:T(8,128)S(1)} %copy-done.15, f32[1024]{0:T(1024)S(1)} %copy-done.113, f32[1024,1024]{0,1:T(8,128)} %copy-done.184), kind=kOutput, calls=%fused_computation.82 | convolution fusion | flops 19922944 | bytes 8400896 | tf_op jit(solution)/shard_map/transpose(jvp())/dot_general | solution.py:55
  436.4 4.6 collective-permute-start.8
  442.4 4.4 collective-permute-done.9
  446.8 4.6 collective-permute-start.10
  452.7 41.9 %all-reduce.40 = (f32[8,1024]{1,0:T(8,128)}, f32[9,64]{1,0:T(8,128)}, f32[1024]{0:T(1024)}, f32[64]{0:T(128)}, f32[64]{0:T(128)}) all-reduce(f32[8,1024]{1,0:T(8,128)S(1)} %fusion.114, f32[9,64]{1,0:T(8,128)S(1)} %bitcast.393, f32[1024]{0:T(1024)S(1)} %bitcast.396, ...), channel_id=1, replica_groups=mesh['gx'=4,'gy'=4,'gz'=2] {'gx','gy','gz'}, use_global_device_ids=true, to_apply=%region_31.32 | all-reduce | flops 9920 | bytes 79360 | tf_op jit(solution)/shard_map/psum | solution.py:291
  495.1 132.5 %all-reduce.44.cloned.1.call-done = (f32[64,1024]{1,0:T(8,128)}, f32[64,1024]{1,0:T(8,128)}, f32[1024,64]{0,1:T(8,128)}, f32[1,1024,64]{1,2,0:T(8,128)}, f32[1,1...) async-done(((f32[64,1024]{1,0:T(8,128)}, f32[64,1024]{1,0:T(8,128)}, f32[1024,64]{0,1:T(8,128)}, f32[1,1024,64]{1,2,0:T(8,128)}, ...) | async-done | bytes 11272208 | tf_op jit(solution)/shard_map/psum | solution.py:291
  629.5 10.0 %pad_maximum_fusion = f32[2,1216,1024]{2,1,0:T(8,128)} fusion(f32[1,1216,1024]{2,1,0:T(8,128)} %get-tuple-element.46, f32[1,1216,1024]{2,1,0:T(8,128)} %get-tuple-element.47), kind=kLoop, calls=%fused_computation.3 | loop fusion | flops 2490368 | bytes 19922944 | tf_op jit(solution)/shard_map/stack | solution.py:305
  (529 shorter events, 84.9 us)
Async XLA Ops:
  7.2 56.5 %copy-start = (f32[1024,64]{0,1:T(8,128)S(1)}, f32[1024,64]{0,1:T(8,128)}, u32[]{:S(2)}) copy-start(f32[1024,64]{0,1:T(8,128)} %param.23) | copy-start | bytes 786436
  7.2 23.2 %copy-start.171 = (s32[32]{0:T(128)S(1)}, s32[32]{0:T(128)}, u32[]{:S(2)}) copy-start(s32[32]{0:T(128)} %param.18) | copy-start | bytes 388
  7.2 23.2 %copy-start.178 = (f32[32]{0:T(128)S(1)}, f32[32]{0:T(128)}, u32[]{:S(2)}) copy-start(f32[32]{0:T(128)} %param.30) | copy-start | bytes 388
  7.2 23.2 %copy-start.176 = (f32[64]{0:T(128)S(1)}, f32[64]{0:T(128)}, u32[]{:S(2)}) copy-start(f32[64]{0:T(128)} %param.28) | copy-start | bytes 772
  7.2 620.4 %all-reduce.44.cloned.1.call-start = ((), (), s32[]{:S(2)}) async-start(), calls=%async_computation | async-start | bytes 22544384 | tf_op jit(solution)/shard_map/psum | solution.py:291
  8.7 15.6 %collective-permute-start.1 = (f32[4,1,1,1,32]{4,0,3,2,1:T(4,128)S(1)}, f32[4,1,1,1,32]{4,0,3,2,1:T(4,128)S(1)}, u32[]{:S(2)}, u32[]{:S(2)}) collective-permute-start(f32[4,1,1,1,32]{4,0,3,2,1:T(4,128)S(1)} %maximum_bitcast_fusion), channel_id=1, source_target_pairs={{8,0},{16,8},{24,16},{9,1},{17,9},{25,17},{10,2},{18,10},{26,18},{... | collective-permute-start | bytes 1544 | tf_op jit(solution)/shard_map/ppermute | solution.py:47
  9.9 14.3 %collective-permute-start = (f32[4,1,1,1,32]{4,0,3,2,1:T(4,128)S(1)}, f32[4,1,1,1,32]{4,0,3,2,1:T(4,128)S(1)}, u32[]{:S(2)}, u32[]{:S(2)}) collective-permute-start(f32[4,1,1,1,32]{4,0,3,2,1:T(4,128)S(1)} %maximum_bitcast_fusion), channel_id=1, source_target_pairs={{0,8},{8,16},{16,24},{1,9},{9,17},{17,25},{2,10},{10,18},{18,26},{... | collective-permute-start | bytes 1544 | tf_op jit(solution)/shard_map/ppermute | solution.py:45
  16.2 15.5 %copy-start.109 = (s32[1024,1]{0,1:T(1,128)}, s32[1024,1]{0,1:T(1,128)S(1)}, u32[]{:S(2)}) copy-start(s32[1024,1]{0,1:T(1,128)S(1)} %compare_select_fusion) | copy-start | bytes 12292
  18.6 13.1 %copy-start.107 = (s32[1024]{0:T(1024)}, s32[1024]{0:T(1024)S(1)}, u32[]{:S(2)}) copy-start(s32[1024]{0:T(1024)S(1)} %eq.44) | copy-start | bytes 12292
  19.3 17.5 %copy-start.116 = (pred[32,32]{1,0:T(8,128)(4,1)}, pred[32,32]{1,0:T(8,128)(4,1)S(1)}, u32[]{:S(2)}) copy-start(pred[32,32]{1,0:T(8,128)(4,1)S(1)} %get-tuple-element.62) | copy-start | bytes 3076
  19.3 25.9 %copy-start.130 = (f32[3]{0:T(128)S(1)}, f32[3]{0:T(128)}, u32[]{:S(2)}) copy-start(f32[3]{0:T(128)} %constant.49.clone) | copy-start | bytes 40
  19.3 27.4 %copy-start.126 = (f32[5,3,3]{0,2,1:T(4,128)S(1)}, f32[5,3,3]{0,2,1:T(4,128)}, u32[]{:S(2)}) copy-start(f32[5,3,3]{0,2,1:T(4,128)} %constant.50.clone) | copy-start | bytes 544
  24.2 23.2 %copy-start.94 = (f32[64,1024]{1,0:T(8,128)S(1)}, f32[64,1024]{1,0:T(8,128)}, u32[]{:S(2)}) copy-start(f32[64,1024]{1,0:T(8,128)} %param.21) | copy-start | bytes 786436
  24.3 6.8 %collective-permute-start.3 = (f32[4,3,1,1,32]{4,0,3,2,1:T(4,128)S(1)}, f32[4,3,1,1,32]{4,0,3,2,1:T(4,128)S(1)}, u32[]{:S(2)}, u32[]{:S(2)}) collective-permute-start(f32[4,3,1,1,32]{4,0,3,2,1:T(4,128)S(1)} %pad_maximum_fusion.19), channel_id=1, source_target_pairs={{2,0},{4,2},{6,4},{3,1},{5,3},{7,5},{10,8},{12,10},{14,12},{11,9},... | collective-permute-start | bytes 4616 | tf_op jit(solution)/shard_map/ppermute | solution.py:47
  25.7 6.0 collective-permute-start.2
  31.7 4.6 collective-permute-start.5
  33.0 3.9 collective-permute-start.4
  36.1 13.4 %copy-start.166 = (f32[8]{0:T(128)}, f32[8]{0:T(128)S(1)}, u32[]{:S(2)}) copy-start(f32[8]{0:T(128)S(1)} %convert_multiply_fusion) | copy-start | bytes 100
  36.2 13.3 %copy-start.114 = (f32[1024]{0:T(1024)}, f32[1024]{0:T(1024)S(1)}, u32[]{:S(2)}) copy-start(f32[1024]{0:T(1024)S(1)} %reshape.706) | copy-start | bytes 12292
  36.3 13.1 %copy-start.103 = (f32[1024]{0:T(1024)}, f32[1024]{0:T(1024)S(1)}, u32[]{:S(2)}) copy-start(f32[1024]{0:T(1024)S(1)} %reshape.700) | copy-start | bytes 12292
  85.5 21.5 %copy-start.88 = (f32[3,64,1024]{2,1,0:T(8,128)}, f32[3,64,1024]{2,1,0:T(8,128)S(1)}, u32[]{:S(2)}) copy-start(f32[3,64,1024]{2,1,0:T(8,128)S(1)} %pad_maximum_fusion.7) | copy-start | bytes 2359300
  85.5 23.5 %copy-start.66 = (f32[2,1024,64]{1,2,0:T(8,128)S(1)}, f32[2,1024,64]{1,2,0:T(8,128)}, u32[]{:S(2)}) copy-start(f32[2,1024,64]{1,2,0:T(8,128)} %param.24) | copy-start | bytes 1572868
  174.2 20.8 %copy-start.155 = (f32[1024]{0:T(1024)S(1)}, f32[1024]{0:T(1024)}, u32[]{:S(2)}) copy-start(f32[1024]{0:T(1024)} %get-tuple-element.152) | copy-start | bytes 12292
  174.2 41.8 %slice-start.2 = ((s8[9961472]{0:T(1024)(128)(4,1)}), s8[4194304]{0:T(1024)(128)(4,1)S(1)}, s32[]{:S(2)}) async-start(s8[9961472]{0:T(1024)(128)(4,1)} %bitcast.406), calls=%async_computation.3 | async-start | bytes 8388608
  174.2 41.8 %slice-start.3 = ((s8[9961472]{0:T(1024)(128)(4,1)}), s8[4194304]{0:T(1024)(128)(4,1)S(1)}, s32[]{:S(2)}) async-start(s8[9961472]{0:T(1024)(128)(4,1)} %bitcast.406), calls=%async_computation.4 | async-start | bytes 8388608
  194.9 21.0 %copy-start.184 = (f32[1024,1024]{0,1:T(8,128)}, f32[1024,1024]{0,1:T(8,128)S(1)}, u32[]{:S(2)}) copy-start(f32[1024,1024]{0,1:T(8,128)S(1)} %get-tuple-element.167) | copy-start | bytes 12582916
  195.0 21.1 %slice-start.4 = ((s8[9961472]{0:T(1024)(128)(4,1)}), s8[1572864]{0:T(1024)(128)(4,1)S(1)}, s32[]{:S(2)}) async-start(s8[9961472]{0:T(1024)(128)(4,1)} %bitcast.406), calls=%async_computation.5 | async-start | bytes 3145728
  259.4 11.7 %copy-start.67 = (f32[2,1024,64]{1,2,0:T(8,128)S(1)}, f32[2,1024,64]{1,2,0:T(8,128)}, u32[]{:S(2)}) copy-start(f32[2,1024,64]{1,2,0:T(8,128)} %param.24) | copy-start | bytes 1572868
  259.4 11.7 %copy-start.158 = (f32[1024]{0:T(1024)S(1)}, f32[1024]{0:T(1024)}, u32[]{:S(2)}) copy-start(f32[1024]{0:T(1024)} %mul.1198) | copy-start | bytes 12292
  259.4 11.7 %copy-start.174 = (f32[1024]{0:T(1024)S(1)}, f32[1024]{0:T(1024)}, u32[]{:S(2)}) copy-start(f32[1024]{0:T(1024)} %param.27) | copy-start | bytes 12292
  259.4 11.7 %copy-start.183 = (f32[1024,1024]{0,1:T(8,128)S(1)}, f32[1024,1024]{0,1:T(8,128)}, u32[]{:S(2)}) copy-start(f32[1024,1024]{0,1:T(8,128)} %get-tuple-element.159) | copy-start | bytes 12582916
  271.1 28.5 %slice-start.5 = ((s8[9961472]{0:T(1024)(128)(4,1)}), s8[4194304]{0:T(1024)(128)(4,1)S(1)}, s32[]{:S(2)}) async-start(s8[9961472]{0:T(1024)(128)(4,1)} %bitcast.408), calls=%async_computation.6 | async-start | bytes 8388608
  271.2 28.5 %slice-start.6 = ((s8[9961472]{0:T(1024)(128)(4,1)}), s8[4194304]{0:T(1024)(128)(4,1)S(1)}, s32[]{:S(2)}) async-start(s8[9961472]{0:T(1024)(128)(4,1)} %bitcast.408), calls=%async_computation.7 | async-start | bytes 8388608
  278.8 20.9 %copy-start.182 = (f32[1024,1024]{0,1:T(8,128)}, f32[1024,1024]{0,1:T(8,128)S(1)}, u32[]{:S(2)}) copy-start(f32[1024,1024]{0,1:T(8,128)S(1)} %get-tuple-element.165) | copy-start | bytes 12582916
  278.8 20.9 %slice-start.7 = ((s8[9961472]{0:T(1024)(128)(4,1)}), s8[1572864]{0:T(1024)(128)(4,1)S(1)}, s32[]{:S(2)}) async-start(s8[9961472]{0:T(1024)(128)(4,1)} %bitcast.408), calls=%async_computation.8 | async-start | bytes 3145728
  299.7 18.1 %copy-start.47 = (f32[1,64,1024]{2,1,0:T(8,128)S(1)}, f32[1,64,1024]{2,1,0:T(8,128)}, u32[]{:S(2)}) copy-start(f32[1,64,1024]{2,1,0:T(8,128)} %get-tuple-element.50) | copy-start | bytes 786436
  299.7 18.1 %copy-start.134 = (f32[64]{0:T(128)S(1)}, f32[64]{0:T(128)}, u32[]{:S(2)}) copy-start(f32[64]{0:T(128)} %get-tuple-element.139) | copy-start | bytes 772
  299.8 20.0 %copy-start.129 = (f32[5,3,3,1]{0,1,2,3:T(4,128)S(1)}, f32[5,3,3,1]{0,1,2,3:T(4,128)}, u32[]{:S(2)}) copy-start(f32[5,3,3,1]{0,1,2,3:T(4,128)} %constant.138) | copy-start | bytes 544
  317.8 11.2 %copy-start.102 = (f32[1024,1216]{0,1:T(8,128)}, f32[1024,1216]{0,1:T(8,128)S(1)}, u32[]{:S(2)}) copy-start(f32[1024,1216]{0,1:T(8,128)S(1)} %fusion.11) | copy-start | bytes 14942212
  366.1 10.9 %copy-start.28 = (f32[5,64,1024]{2,1,0:T(8,128)S(1)}, f32[5,64,1024]{2,1,0:T(8,128)}, u32[]{:S(2)}) copy-start(f32[5,64,1024]{2,1,0:T(8,128)} %get-tuple-element.83) | copy-start | bytes 3932164
  366.1 10.9 %copy-start.29 = (f32[5,64,1024]{2,1,0:T(8,128)S(1)}, f32[5,64,1024]{2,1,0:T(8,128)}, u32[]{:S(2)}) copy-start(f32[5,64,1024]{2,1,0:T(8,128)} %get-tuple-element.101) | copy-start | bytes 3932164
  366.1 10.9 %copy-start.43 = (f32[3,64,1024]{2,1,0:T(8,128)S(1)}, f32[3,64,1024]{2,1,0:T(8,128)}, u32[]{:S(2)}) copy-start(f32[3,64,1024]{2,1,0:T(8,128)} %get-tuple-element.65) | copy-start | bytes 2359300
  366.2 10.9 %copy-start.44 = (f32[3,64,1024]{2,1,0:T(8,128)S(1)}, f32[3,64,1024]{2,1,0:T(8,128)}, u32[]{:S(2)}) copy-start(f32[3,64,1024]{2,1,0:T(8,128)} %get-tuple-element.113) | copy-start | bytes 2359300
  366.2 10.9 %copy-start.54 = (f32[64,1024]{1,0:T(8,128)S(1)}, f32[64,1024]{1,0:T(8,128)}, u32[]{:S(2)}) copy-start(f32[64,1024]{1,0:T(8,128)} %convolution_bitcast_fusion.6) | copy-start | bytes 786436
  404.8 17.9 %copy-start.177 = (f32[64]{0:T(128)S(1)}, f32[64]{0:T(128)}, u32[]{:S(2)}) copy-start(f32[64]{0:T(128)} %param.29) | copy-start | bytes 772
  404.8 17.9 %copy-start.180 = (f32[32]{0:T(128)S(1)}, f32[32]{0:T(128)}, u32[]{:S(2)}) copy-start(f32[32]{0:T(128)} %get-tuple-element.155) | copy-start | bytes 388
  410.7 18.5 %copy-start.154 = (f32[1024]{0:T(1024)S(1)}, f32[1024]{0:T(1024)}, u32[]{:S(2)}) copy-start(f32[1024]{0:T(1024)} %get-tuple-element.148) | copy-start | bytes 12292
  418.1 11.1 %copy-start.15 = (f32[1024,1024]{0,1:T(8,128)S(1)}, f32[1024,1024]{0,1:T(8,128)}, u32[]{:S(2)}) copy-start(f32[1024,1024]{0,1:T(8,128)} %copy-done.12) | copy-start | bytes 12582916
  418.1 18.2 %collective-permute-start.7 = (f32[3,3,3,1,32]{4,0,3,2,1:T(4,128)S(1)}, f32[3,3,3,1,32]{4,0,3,2,1:T(4,128)S(1)}, u32[]{:S(2)}, u32[]{:S(2)}) collective-permute-start(f32[3,3,3,1,32]{4,0,3,2,1:T(4,128)S(1)} %copy.379), channel_id=1, source_target_pairs={{1,0},{3,2},{5,4},{7,6},{9,8},{11,10},{13,12},{15,14},{17,16},{19,... | collective-permute-start | bytes 10376 | tf_op jit(solution)/shard_map/ppermute | solution.py:34
  419.7 16.7 %collective-permute-start.6 = (f32[3,3,3,1,32]{4,0,3,2,1:T(4,128)S(1)}, f32[3,3,3,1,32]{4,0,3,2,1:T(4,128)S(1)}, u32[]{:S(2)}, u32[]{:S(2)}) collective-permute-start(f32[3,3,3,1,32]{4,0,3,2,1:T(4,128)S(1)} %copy.378), channel_id=1, source_target_pairs={{0,1},{2,3},{4,5},{6,7},{8,9},{10,11},{12,13},{14,15},{16,17},{18,... | collective-permute-start | bytes 10376 | tf_op jit(solution)/shard_map/ppermute | solution.py:34
  429.3 13.1 %copy-start.159 = (f32[64]{0:T(128)S(1)}, f32[64]{0:T(128)}, u32[]{:S(2)}) copy-start(f32[64]{0:T(128)} %get-tuple-element.27) | copy-start | bytes 772
  429.3 13.1 %copy-start.160 = (f32[64]{0:T(128)S(1)}, f32[64]{0:T(128)}, u32[]{:S(2)}) copy-start(f32[64]{0:T(128)} %get-tuple-element.28) | copy-start | bytes 772
  429.3 13.1 %copy-start.161 = (f32[64]{0:T(128)S(1)}, f32[64]{0:T(128)}, u32[]{:S(2)}) copy-start(f32[64]{0:T(128)} %get-tuple-element.84) | copy-start | bytes 772
  429.3 13.1 %copy-start.162 = (f32[64]{0:T(128)S(1)}, f32[64]{0:T(128)}, u32[]{:S(2)}) copy-start(f32[64]{0:T(128)} %get-tuple-element.87) | copy-start | bytes 772
  429.3 13.1 %copy-start.164 = (f32[64]{0:T(128)S(1)}, f32[64]{0:T(128)}, u32[]{:S(2)}) copy-start(f32[64]{0:T(128)} %get-tuple-element.20) | copy-start | bytes 772
  429.3 13.1 %copy-start.165 = (f32[64]{0:T(128)S(1)}, f32[64]{0:T(128)}, u32[]{:S(2)}) copy-start(f32[64]{0:T(128)} %get-tuple-element.21) | copy-start | bytes 772
  429.3 13.1 %copy-start.168 = (f32[64]{0:T(128)S(1)}, f32[64]{0:T(128)}, u32[]{:S(2)}) copy-start(f32[64]{0:T(128)} %get-tuple-element.22) | copy-start | bytes 772
  429.3 13.1 %copy-start.169 = (f32[64]{0:T(128)S(1)}, f32[64]{0:T(128)}, u32[]{:S(2)}) copy-start(f32[64]{0:T(128)} %get-tuple-element.24) | copy-start | bytes 772
  429.3 13.1 %copy-start.170 = (f32[64]{0:T(128)S(1)}, f32[64]{0:T(128)}, u32[]{:S(2)}) copy-start(f32[64]{0:T(128)} %get-tuple-element.26) | copy-start | bytes 772
  436.4 6.0 collective-permute-start.8
  441.0 5.8 collective-permute-start.9
  446.8 47.7 %collective-permute-start.10 = (f32[3,1,1,1,32]{4,0,3,2,1:T(4,128)S(1)}, f32[3,1,1,1,32]{4,0,3,2,1:T(4,128)S(1)}, u32[]{:S(2)}, u32[]{:S(2)}) collective-permute-start(f32[3,1,1,1,32]{4,0,3,2,1:T(4,128)S(1)} %get-tuple-element.142), channel_id=1, source_target_pairs={{0,8},{8,16},{16,24},{1,9},{9,17},{17,25},{2,10},{10,18},{18,26},{... | collective-permute-start | bytes 1160 | tf_op jit(solution)/shard_map/ppermute | solution.py:34
  451.4 43.2 %collective-permute-start.11 = (f32[3,1,1,1,32]{4,0,3,2,1:T(4,128)S(1)}, f32[3,1,1,1,32]{4,0,3,2,1:T(4,128)S(1)}, u32[]{:S(2)}, u32[]{:S(2)}) collective-permute-start(f32[3,1,1,1,32]{4,0,3,2,1:T(4,128)S(1)} %get-tuple-element.143), channel_id=1, source_target_pairs={{8,0},{16,8},{24,16},{9,1},{17,9},{25,17},{10,2},{18,10},{26,18},{... | collective-permute-start | bytes 1160 | tf_op jit(solution)/shard_map/ppermute | solution.py:34
  629.5 11.4 %copy-start.97 = (f32[1024,64]{0,1:T(8,128)S(1)}, f32[1024,64]{0,1:T(8,128)}, u32[]{:S(2)}) copy-start(f32[1024,64]{0,1:T(8,128)} %get-tuple-element.177) | copy-start | bytes 786436
  (142 other events, 682.6 us)
Sparse Core Ops, SparseCore 0:
  398.7 228.9 all-reduce.43
where the time goes:
time: 654 us; the launch traced here: 649 us
  matrix products  250 us (38%)
  waiting for transfers between devices  138 us (21%)
  other arithmetic  84.8 us (13%)
  local copies, waits for them, and re-layouts  83.1 us (13%)
  blocking collectives  41.9 us (6%)
  starting transfers between devices  33.5 us (5%)
  between operations  16.9 us (3%)
    dot_general x28, matrix products, product(): jnp.dot(left_side, right_side, precision=PRECISE, preferred_element_type=...  219 us
    psum x1, waiting for transfers between devices, per_device(): lax.psum((d_env_early, d_lat_early, d_path, d_center, d_neigh, d_radial,...  132 us
    psum x1, blocking collectives, per_device(): lax.psum((d_env_early, d_lat_early, d_path, d_center, d_neigh, d_radial,...  41.9 us
    broadcast_in_dim x15, local copies, waits for them, and re-layouts, environment(): jnp.broadcast_to(summed[:, :, None, :], (9, CHANNELS, NB, atom_count))  23.8 us
    ppermute x6, starting transfers between devices, shifted(): return lax.ppermute(value, axis, pairs)  16.3 us
    dot_general x2, matrix products, couple(): jnp.einsum('mik,mcn,kcn->icn', harmonic_basis, tensor_part, env_vector, p...  16.1 us
    dot_general x2, matrix products, couple(): jnp.einsum('mik,icn,kcn->mcn', harmonic_basis, vector_part, env_vector, p...  14.7 us
    ppermute x3, starting transfers between devices, with_halo(): lax.ppermute(tail, axis, [(i, (i + 1) % count) for i in range(ends)])  13.1 us
  transfers between devices with their start and end apart: 13, of which 4 were waited for; matrix products, arithmetic and copies ran while one was open for 7% of the time, Pallas kernels for 0%

commit v1 on v0

v1 whole, which is shorter than its diff:
```python
import functools
import math

import jax
import jax.numpy as jnp
import numpy as np
from jax import lax
from jax.experimental import pallas as pl
from jax.experimental.pallas import tpu as pltpu
from jax.sharding import PartitionSpec as P

LATENT = 1024
CHANNELS = 64
NSPEC = 64
NBESSEL = 8
NB = 32
ATOMS = 32
EDGES = NB * ATOMS
WIDE = LATENT + 3 * CHANNELS
HALF = LATENT // 2
QUARTER = LATENT // 4
NTAB = 27 * ATOMS
OWN = 13 * ATOMS

CUTOFF = 5.0
RH = 0.7071067811865476
HR = 0.7071067811865476
SR = 0.4082482904638631
R3 = math.sqrt(3.0)
Q75 = math.sqrt(7.5)
NORM = NB**-0.5
BESSEL = math.sqrt(2.0 / CUTOFF)

F32 = jnp.float32
BF16 = jnp.bfloat16

G_SMOOTH, G_LIVE, G_R, G_DISP, G_GRAD, G_RAD, G_GS, G_SPEC = 9, 10, 11, 12, 15, 16, 24, 25
G_ROWS = 32


def dot(a, b, ca, cb):
    return lax.dot_general(a, b, (((ca,), (cb,)), ((), ())), preferred_element_type=F32)


def dot3(ah, al, bh, bl, ca, cb):
    return dot(ah, bh, ca, cb) + dot(ah, bl, ca, cb) + dot(al, bh, ca, cb)


def split(x):
    hi = x.astype(BF16)
    return hi, (x - hi.astype(F32)).astype(BF16)


def pieces(x):
    hi = x.astype(BF16).astype(F32)
    rest = x - hi
    mid = rest.astype(BF16).astype(F32)
    return hi, mid, rest - mid


def sigmoid(x):
    return 0.5 * jnp.tanh(0.5 * x) + 0.5


def silu_both(x):
    sig = sigmoid(x)
    return x * sig, sig * (1.0 + x * (1.0 - sig))


def lanes(i, width):
    return pl.ds(pl.multiple_of(i * width, width), width)


def over(count, body):
    def step(i, carry):
        body(i)
        return carry

    lax.fori_loop(0, count, step, 0)


def iota(shape, dim):
    return lax.broadcasted_iota(jnp.int32, shape, dim)


def slot_total(x):
    x = x + pltpu.roll(x, 64, 1)
    return x + pltpu.roll(x, 32, 1)


def make_env(geo, w, env):
    for c in range(9):
        acc = None
        for k in range(8):
            cols = pl.ds(k * 128, 128)
            term = w[:, cols] if c == 0 else geo[c : c + 1, cols] * w[:, cols]
            acc = term if acc is None else acc + term
        env[c * 64 : (c + 1) * 64, :] = slot_total(acc) * NORM


def rows_of(ref, c, cols=slice(None)):
    return ref[c * 64 : (c + 1) * 64, cols]


def fwd_kernel(
    tab, slots, cent, w0h, w0l, ec, en, rad_w, ve, ev, path, scale,
    x0h, x0l, x1h, x1l, z0, pre, vw, w1, geo, g0, g1, f1,
    gat, table, veh, vel, evh, evl,
):
    hi, mid, lo = pieces(tab[...])
    tab24 = jnp.concatenate([hi, mid, lo], 0).astype(BF16)

    def gather(i):
        cols = lanes(i, 256)
        hot = jnp.where(iota((NTAB, 256), 0) == slots[:, cols], 1.0, 0.0).astype(BF16)
        got = dot(tab24, hot, 1, 0)
        gat[:, cols] = got[0:8] + got[8:16] + got[16:24]

    over(4, gather)

    live = jnp.where(slots[...] != OWN + iota((1, EDGES), 1) % ATOMS, 1.0, 0.0)
    dead = 1.0 - live
    dx = (gat[0:1, :] - cent[0:1, :]) * live + dead * 2.5
    dy = (gat[1:2, :] - cent[1:2, :]) * live
    dz = (gat[2:3, :] - cent[2:3, :]) * live
    r = jnp.sqrt(dx * dx + dy * dy + dz * dz)
    inv = 1.0 / r
    t = r / CUTOFF
    t2 = t * t
    t6 = t2 * t2 * t2
    smooth = live * (1.0 - 28.0 * t6 + 48.0 * t6 * t - 21.0 * t6 * t * t)
    ux, uy, uz = dx * inv, dy * inv, dz * inv
    geo[0:1, :] = jnp.ones_like(r)
    geo[1:2, :] = R3 * ux
    geo[2:3, :] = R3 * uy
    geo[3:4, :] = R3 * uz
    geo[4:5, :] = Q75 * HR * (ux * ux - uy * uy)
    geo[5:6, :] = Q75 * SR * (ux * ux + uy * uy - 2.0 * uz * uz)
    geo[6:7, :] = Q75 * 2.0 * HR * (ux * uy)
    geo[7:8, :] = Q75 * 2.0 * HR * (ux * uz)
    geo[8:9, :] = Q75 * 2.0 * HR * (uy * uz)
    geo[9:10, :] = smooth
    geo[10:11, :] = live
    geo[11:12, :] = r
    geo[12:13, :] = dx
    geo[13:14, :] = dy
    geo[14:15, :] = dz
    order = (iota((8, EDGES), 0) + 1).astype(F32) * (math.pi / CUTOFF)
    geo[16:24, :] = smooth * BESSEL * jnp.sin(order * r) * inv
    hot_c = jnp.where(iota((NSPEC, EDGES), 0).astype(F32) == cent[3:4, :], 1.0, 0.0)
    grad = cent[4:5, :] * jnp.sum(hot_c * scale[...], 0, keepdims=True)
    geo[15:16, :] = grad
    geo[24:25, :] = grad * smooth
    geo[25:26, :] = gat[3:4, :]
    geo[26:32, :] = jnp.zeros((6, EDGES), F32)

    ech, ecl = split(ec[...])
    enh, enl = split(en[...])
    rh = rad_w[...].astype(BF16).astype(F32)
    rl = rad_w[...] - rh
    table[0:64, :] = ech
    table[64:128, :] = enh
    table[128:192, :] = ecl
    table[192:256, :] = enl
    table[256:288, :] = jnp.concatenate([rh, rl, rh, jnp.zeros_like(rh)], 0).astype(BF16)
    veh[...], vel[...] = split(ve[...])
    evh[...], evl[...] = split(ev[...])

    def embed(i):
        cols = lanes(i, 256)
        kinds = iota((NSPEC, 256), 0).astype(F32)
        hot_c = jnp.where(kinds == cent[3:4, cols], 1.0, 0.0)
        hot_n = jnp.where(kinds == gat[3:4, cols], 1.0, 0.0)
        hots = jnp.concatenate([hot_c, hot_n], 0).astype(BF16)
        rad = geo[16:24, cols]
        rad_h = rad.astype(BF16).astype(F32)
        rads = jnp.concatenate([rad_h, rad_h, rad - rad_h, jnp.zeros_like(rad)], 0).astype(BF16)
        pre[:, cols] = dot(table[...], jnp.concatenate([hots, hots, rads], 0), 0, 0)
        sm = geo[9:10, cols]
        for b in range(8):
            rows = pl.ds(b * 128, 128)
            p = pre[rows, cols]
            x0h[rows, cols], x0l[rows, cols] = split(p * sigmoid(p) * sm)
        vw[:, cols] = dot3(
            veh[...], vel[...], x0h[0:LATENT, cols], x0l[0:LATENT, cols], 0, 0
        )

    over(4, embed)
    make_env(geo, vw.at[64:128, :], g0)

    def tensor(k):
        cols = lanes(k, 128)
        v = vw[0:64, cols]
        y = [geo[c : c + 1, cols] for c in range(9)]
        e0 = rows_of(g0, 0)
        e1, e2, e3 = rows_of(g0, 1), rows_of(g0, 2), rows_of(g0, 3)
        a, b, c = y[1] * e1, y[2] * e2, y[3] * e3
        vec = a + b + c
        quad = y[4] * rows_of(g0, 4)
        for m in range(5, 9):
            quad = quad + y[m] * rows_of(g0, m)
        x0h[1024:1088, cols], x0l[1024:1088, cols] = split(v * e0)
        x0h[1088:1152, cols], x0l[1088:1152, cols] = split(v * vec)
        x0h[1152:1216, cols], x0l[1152:1216, cols] = split(v * quad)
        p = [rows_of(path, n) for n in range(9)]
        e12, e13 = y[1] * e2, y[1] * e3
        e21, e23 = y[2] * e1, y[2] * e3
        e31, e32 = y[3] * e1, y[3] * e2
        q00 = HR * y[4] + SR * y[5]
        q11 = SR * y[5] - HR * y[4]
        q22 = -2.0 * SR * y[5]
        q01, q02, q12 = HR * y[6], HR * y[7], HR * y[8]
        f1[0:64, cols] = v * (p[0] * e0 + p[1] * vec)
        p3g = p[3] * e0
        f1[64:128, cols] = v * (
            p[2] * e1 + p3g * y[1] + p[4] * (e23 - e32) + p[5] * (q00 * e1 + q01 * e2 + q02 * e3)
        )
        f1[128:192, cols] = v * (
            p[2] * e2 + p3g * y[2] + p[4] * (e31 - e13) + p[5] * (q01 * e1 + q11 * e2 + q12 * e3)
        )
        f1[192:256, cols] = v * (
            p[2] * e3 + p3g * y[3] + p[4] * (e12 - e21) + p[5] * (q02 * e1 + q12 * e2 + q22 * e3)
        )
        p8g = p[8] * e0
        pair = (
            HR * (a - b),
            SR * (a + b - 2.0 * c),
            HR * (e12 + e21),
            HR * (e13 + e31),
            HR * (e23 + e32),
        )
        for m in range(5):
            f1[(4 + m) * 64 : (5 + m) * 64, cols] = v * (
                p[6] * pair[m] + p[7] * rows_of(g0, 4 + m) + p8g * y[4 + m]
            )

    over(8, tensor)

    def layer(i):
        cols = lanes(i, 256)
        z0[:, cols] = dot3(w0h[...], w0l[...], x0h[:, cols], x0l[:, cols], 0, 0)
        sm = geo[9:10, cols]
        for b in range(8):
            rows = pl.ds(b * 128, 128)
            z = z0[rows, cols]
            old = x0h[rows, cols].astype(F32) + x0l[rows, cols].astype(F32)
            x1h[rows, cols], x1l[rows, cols] = split((old + sm * (z * sigmoid(z))) * RH)
        w1[:, cols] = dot3(
            evh[...], evl[...], x1h[0:LATENT, cols], x1l[0:LATENT, cols], 0, 0
        )

    over(4, layer)
    make_env(geo, w1, g1)

    def scalars(k):
        cols = lanes(k, 128)
        s0 = rows_of(f1, 0, cols) * rows_of(g1, 0)
        s1 = rows_of(f1, 1, cols) * rows_of(g1, 1)
        for c in range(2, 4):
            s1 = s1 + rows_of(f1, c, cols) * rows_of(g1, c)
        s2 = rows_of(f1, 4, cols) * rows_of(g1, 4)
        for c in range(5, 9):
            s2 = s2 + rows_of(f1, c, cols) * rows_of(g1, c)
        x1h[1024:1088, cols], x1l[1024:1088, cols] = split(s0)
        x1h[1088:1152, cols], x1l[1088:1152, cols] = split(s1)
        x1h[1152:1216, cols], x1l[1152:1216, cols] = split(s2)

    over(8, scalars)


def weight_grad(core, xh, xl, qh, ql, keep, send):
    for out, block in ((send, 1 - core), (keep, core)):
        rows = pl.ds(pl.multiple_of(block * QUARTER, QUARTER), QUARTER)
        out[...] = dot3(xh[...], xl[...], qh[rows, :], ql[rows, :], 1, 1)


def late_kernel(half, core, x1h, x1l, wh, wl, outw, geo, qh, ql, keep, send, side, dout, acc):
    wcols = slice(half * HALF, (half + 1) * HALF)
    acc[...] = jnp.zeros_like(acc)
    side[...] = jnp.zeros_like(side)

    def step(i):
        cols = lanes(i, 256)
        z = dot3(wh[:, wcols], wl[:, wcols], x1h[:, cols], x1l[:, cols], 0, 0)
        sm = geo[9:10, cols]
        gs = geo[24:25, cols]
        scale = gs * sm * RH
        reach = jnp.zeros((8, 256), F32)
        total = jnp.zeros((8, 256), F32)
        for b in range(4):
            rows = pl.ds(b * 128, 128)
            frows = pl.ds(half * HALF + b * 128, 128)
            si, dsi = silu_both(z[b * 128 : (b + 1) * 128])
            ow = outw[frows, :]
            qh[rows, cols], ql[rows, cols] = split((ow * scale) * dsi)
            lat = (
                x1h[frows, cols].astype(F32) + x1l[frows, cols].astype(F32) + sm * si
            ) * RH
            part = gs * lat
            acc[rows, :] += part[:, 0:128] + part[:, 128:256]
            reach = reach + jnp.sum((ow * si).reshape(16, 8, 256), 0)
            total = total + jnp.sum((ow * lat).reshape(16, 8, 256), 0)
        side[0:1, cols] = jnp.sum(reach, 0, keepdims=True)
        side[1:2, cols] = jnp.sum(total, 0, keepdims=True)

    over(4, step)
    dout[...] = jnp.broadcast_to(jnp.sum(acc[...].T, 0, keepdims=True), dout.shape)
    weight_grad(core[0], x1h, x1l, qh, ql, keep, send)


def mid_kernel(qah, qal, qbh, qbl, wh, wl, f1, g1, w1, geo, ds1, dwh, dwl, dy, denv):
    def scal(i):
        cols = lanes(i, 256)
        ds1[:, cols] = dot3(
            wh[1024:1216, 0:512], wl[1024:1216, 0:512], qah[:, cols], qal[:, cols], 1, 0
        ) + dot3(
            wh[1024:1216, 512:1024], wl[1024:1216, 512:1024], qbh[:, cols], qbl[:, cols], 1, 0
        )

    over(4, scal)
    for c in range(9):
        kind = 0 if c == 0 else (1 if c < 4 else 2)
        acc = None
        for k in range(8):
            cols = pl.ds(k * 128, 128)
            term = rows_of(ds1, kind, cols) * rows_of(f1, c, cols)
            acc = term if acc is None else acc + term
        denv[c * 64 : (c + 1) * 64, :] = slot_total(acc) * NORM
    env_back(geo, w1, denv, dwh, dwl, dy, None)


def env_back(geo, w, denv, dwh, dwl, dy, more):
    def step(k):
        cols = lanes(k, 128)
        acc = rows_of(denv, 0)
        wk = w[:, cols]
        rows = [jnp.zeros((1, 128), F32)]
        for c in range(1, 9):
            d = rows_of(denv, c)
            acc = acc + geo[c : c + 1, cols] * d
            rows.append(jnp.sum(wk * d, 0, keepdims=True))
        dwh[:, cols], dwl[:, cols] = split(acc)
        for c in range(1, 9):
            if more is None:
                dy[c : c + 1, cols] = rows[c]
            else:
                dy[c : c + 1, cols] = rows[c] + more[c : c + 1, cols]

    over(8, step)


def early_kernel(
    half, core, qah, qal, qbh, qbl, wh, wl, ev, dwh, dwl, outw, geo, z0, x0h, x0l,
    dlat, qh, ql, keep, send, side,
    evh, evl,
):
    base = half * HALF
    evh[...], evl[...] = split(ev[base : base + HALF, :])
    side[...] = jnp.zeros_like(side)

    def step(i):
        cols = lanes(i, 256)
        wr = slice(base, base + HALF)
        d = (
            dot3(wh[wr, 0:512], wl[wr, 0:512], qah[:, cols], qal[:, cols], 1, 0)
            + dot3(wh[wr, 512:1024], wl[wr, 512:1024], qbh[:, cols], qbl[:, cols], 1, 0)
            + dot3(evh[...], evl[...], dwh[:, cols], dwl[:, cols], 1, 0)
        )
        sm = geo[9:10, cols] * RH
        gs = geo[24:25, cols] * RH
        total = jnp.zeros((8, 256), F32)
        for b in range(4):
            rows = pl.ds(b * 128, 128)
            frows = pl.ds(base + b * 128, 128)
            dl = d[b * 128 : (b + 1) * 128] + outw[frows, :] * gs
            dlat[rows, cols] = dl * RH
            si, dsi = silu_both(z0[frows, cols])
            qh[rows, cols], ql[rows, cols] = split(dl * dsi * sm)
            total = total + jnp.sum((dl * si).reshape(16, 8, 256), 0)
        side[0:1, cols] = jnp.sum(total, 0, keepdims=True) * RH

    over(4, step)
    weight_grad(core[0], x0h, x0l, qh, ql, keep, send)


def couple_kernel(
    qah, qal, qbh, qbl, wh, wl, vw, geo, g0, g1, ds1, path, x0h, x0l, x1h, x1l, dw1h, dw1l, dy1,
    dvwh, dvwl, dy, dpath, dve, dev,
    ds0, denv, dyv,
):
    def scal(i):
        cols = lanes(i, 256)
        ds0[:, cols] = dot3(
            wh[1024:1216, 0:512], wl[1024:1216, 0:512], qah[:, cols], qal[:, cols], 1, 0
        ) + dot3(
            wh[1024:1216, 512:1024], wl[1024:1216, 512:1024], qbh[:, cols], qbl[:, cols], 1, 0
        )

    over(4, scal)
    denv[...] = jnp.zeros_like(denv)
    dpath[...] = jnp.zeros_like(dpath)

    def step(k):
        cols = lanes(k, 128)
        v = vw[0:64, cols]
        y = [geo[c : c + 1, cols] for c in range(9)]
        e = [rows_of(g0, c) for c in range(9)]
        p = [rows_of(path, n) for n in range(9)]
        s = [rows_of(ds0, n, cols) for n in range(3)]
        u = [rows_of(ds1, n, cols) for n in range(3)]
        f0 = u[0] * rows_of(g1, 0)
        fv = [u[1] * rows_of(g1, c) for c in range(1, 4)]
        fq = [u[2] * rows_of(g1, c) for c in range(4, 9)]
        yv, yq, ev_, eq = y[1:4], y[4:9], e[1:4], e[4:9]

        def dot_of(a, b):
            out = a[0] * b[0]
            for i in range(1, len(a)):
                out = out + a[i] * b[i]
            return out

        m00 = HR * yq[0] + SR * yq[1]
        m11 = SR * yq[1] - HR * yq[0]
        m22 = -2.0 * SR * yq[1]
        m01, m02, m12 = HR * yq[2], HR * yq[3], HR * yq[4]
        t00 = HR * fq[0] + SR * fq[1]
        t11 = SR * fq[1] - HR * fq[0]
        t22 = (-2.0 * SR) * fq[1]
        t01, t02, t12 = HR * fq[2], HR * fq[3], HR * fq[4]

        te = [
            t00 * ev_[0] + t01 * ev_[1] + t02 * ev_[2],
            t01 * ev_[0] + t11 * ev_[1] + t12 * ev_[2],
            t02 * ev_[0] + t12 * ev_[1] + t22 * ev_[2],
        ]
        ty = [
            t00 * yv[0] + t01 * yv[1] + t02 * yv[2],
            t01 * yv[0] + t11 * yv[1] + t12 * yv[2],
            t02 * yv[0] + t12 * yv[1] + t22 * yv[2],
        ]
        mf = [
            m00 * fv[0] + m01 * fv[1] + m02 * fv[2],
            m01 * fv[0] + m11 * fv[1] + m12 * fv[2],
            m02 * fv[0] + m12 * fv[1] + m22 * fv[2],
        ]
        ef = [
            ev_[1] * fv[2] - ev_[2] * fv[1],
            ev_[2] * fv[0] - ev_[0] * fv[2],
            ev_[0] * fv[1] - ev_[1] * fv[0],
        ]
        fy = [
            fv[1] * yv[2] - fv[2] * yv[1],
            fv[2] * yv[0] - fv[0] * yv[2],
            fv[0] * yv[1] - fv[1] * yv[0],
        ]
        e_fv = dot_of(ev_, fv)
        y_fv = dot_of(yv, fv)
        e_fq = dot_of(eq, fq)
        y_fq = dot_of(yq, fq)
        vec = dot_of(yv, ev_)
        y_te = dot_of(yv, te)
        e_mf = dot_of(ev_, mf)
        y_ef = dot_of(yv, ef)

        grads = (
            e[0] * f0,
            vec * f0,
            e_fv,
            e[0] * y_fv,
            y_ef,
            e_mf,
            y_te,
            e_fq,
            e[0] * y_fq,
        )
        for n in range(9):
            dpath[n * 64 : (n + 1) * 64, :] += v * grads[n]

        p1f = p[1] * f0
        d0 = s[0] * e[0] + p[0] * e[0] * f0 + p[2] * e_fv + p[7] * e_fq
        p3e = p[3] * e[0]
        p8e = p[8] * e[0]
        s1f = s[1] + p1f
        dv = d0
        for i in range(3):
            di = s1f * ev_[i] + p3e * fv[i] + p[4] * ef[i] + p[6] * te[i]
            dv = dv + yv[i] * di
            dyv[1 + i : 2 + i, cols] = jnp.sum(v * di, 0, keepdims=True)
        a, b, c = fv[0] * ev_[0], fv[1] * ev_[1], fv[2] * ev_[2]
        bil = (
            HR * (a - b),
            SR * (a + b - 2.0 * c),
            HR * (fv[0] * ev_[1] + fv[1] * ev_[0]),
            HR * (fv[0] * ev_[2] + fv[2] * ev_[0]),
            HR * (fv[1] * ev_[2] + fv[2] * ev_[1]),
        )
        for m in range(5):
            dm = s[2] * eq[m] + p[5] * bil[m] + p8e * fq[m]
            dv = dv + yq[m] * dm
            dyv[4 + m : 5 + m, cols] = jnp.sum(v * dm, 0, keepdims=True)
        dvwh[0:64, cols], dvwl[0:64, cols] = split(dv)

        denv[0:64, :] += v * (s[0] + p[0] * f0 + p[3] * y_fv + p[8] * y_fq)
        for i in range(3):
            denv[(1 + i) * 64 : (2 + i) * 64, :] += v * (
                s1f * yv[i] + p[2] * fv[i] + p[4] * fy[i] + p[5] * mf[i] + p[6] * ty[i]
            )
        for m in range(5):
            denv[(4 + m) * 64 : (5 + m) * 64, :] += v * (s[2] * yq[m] + p[7] * fq[m])

    over(8, step)
    for c in range(9):
        denv[c * 64 : (c + 1) * 64, :] = slot_total(rows_of(denv, c)) * NORM
    dyv[0:1, :] = jnp.zeros((1, EDGES), F32)
    dyv[...] += dy1[...]
    env_back(geo, vw.at[64:128, :], denv, dvwh.at[64:128, :], dvwl.at[64:128, :], dy, dyv)
    dve[...] = dot3(dvwh[...], dvwl[...], x0h[0:LATENT, :], x0l[0:LATENT, :], 1, 1)
    dev[...] = dot3(dw1h[...], dw1l[...], x1h[0:LATENT, :], x1l[0:LATENT, :], 1, 1)


def last_kernel(
    qah, qal, qbh, qbl, wh, wl, ve, dvwh, dvwl, dla, dlb, pre, geo, slots, cent, rad_w,
    sla, slb, sea, seb, dy, dpath, scale, shift,
    hots_grad, rad_grad, ghost, own, energy, misc,
    veh, vel, qph, qpl, dsm, drad,
):
    veh[...], vel[...] = split(ve[...])
    rwh, rwl = split(jnp.concatenate([rad_w[...], jnp.zeros_like(rad_w)], 0))

    def step(i):
        cols = lanes(i, 256)
        sm = geo[9:10, cols]
        total = jnp.zeros((8, 256), F32)
        for h, dl in ((0, dla), (1, dlb)):
            wr = slice(h * HALF, (h + 1) * HALF)
            d = (
                dot3(wh[wr, 0:512], wl[wr, 0:512], qah[:, cols], qal[:, cols], 1, 0)
                + dot3(wh[wr, 512:1024], wl[wr, 512:1024], qbh[:, cols], qbl[:, cols], 1, 0)
                + dot3(veh[wr, :], vel[wr, :], dvwh[:, cols], dvwl[:, cols], 1, 0)
            )
            for b in range(4):
                rows = pl.ds(b * 128, 128)
                frows = pl.ds(h * HALF + b * 128, 128)
                dd = d[b * 128 : (b + 1) * 128] + dl[rows, cols]
                si, dsi = silu_both(pre[frows, cols])
                qph[frows, cols], qpl[frows, cols] = split(dd * dsi * sm)
                total = total + jnp.sum((dd * si).reshape(16, 8, 256), 0)
        dsm[:, cols] = jnp.sum(total, 0, keepdims=True)
        drad[:, cols] = dot3(rwh, rwl, qph[:, cols], qpl[:, cols], 1, 0)[0:8]

    over(4, step)

    kinds = iota((NSPEC, EDGES), 0).astype(F32)
    hot_c = jnp.where(kinds == cent[3:4, :], 1.0, 0.0)
    hot_n = jnp.where(kinds == geo[25:26, :], 1.0, 0.0)
    hots = jnp.concatenate([hot_c, hot_n], 0).astype(BF16)
    rad = geo[16:24, :]
    rad_h = rad.astype(BF16).astype(F32)
    rads = jnp.concatenate([rad_h, rad - rad_h], 0).astype(BF16)
    left = jnp.concatenate([hots, rads], 0)
    full = dot(left, qph[...], 1, 1)
    rest = dot(left, qpl[...], 1, 1)
    hots_grad[...] = full[0:128] + rest[0:128]
    rad_grad[...] = full[128:136] + full[136:144] + rest[128:136]

    live, r, smooth = geo[10:11, :], geo[11:12, :], geo[9:10, :]
    inv = 1.0 / r
    grad = geo[15:16, :]
    reach = sla[0:1, :] + slb[0:1, :]
    lat_out = sla[1:2, :] + slb[1:2, :]
    order = (iota((8, EDGES), 0) + 1).astype(F32) * (math.pi / CUTOFF)
    angle = order * r
    sine = jnp.sin(angle) * inv
    cosine = jnp.cos(angle) * inv
    dr8 = drad[...]
    d_s = (
        grad * lat_out
        + grad * smooth * RH * reach
        + sea[0:1, :]
        + seb[0:1, :]
        + dsm[...]
        + BESSEL * jnp.sum(dr8 * sine, 0, keepdims=True)
    )
    t = r / CUTOFF
    t2 = t * t
    gap = 1.0 - t
    d_r = d_s * (live * (-168.0 / CUTOFF) * (t2 * t2 * t) * (gap * gap)) + (
        smooth * BESSEL
    ) * jnp.sum(dr8 * (order * cosine - sine * inv), 0, keepdims=True)
    ux, uy, uz = geo[12:13, :] * inv, geo[13:14, :] * inv, geo[14:15, :] * inv
    yy = [dy[c : c + 1, :] for c in range(9)]
    h2, s2 = 2.0 * HR * Q75, 2.0 * SR * Q75
    gx = R3 * yy[1] + ux * (h2 * yy[4] + s2 * yy[5]) + h2 * (uy * yy[6] + uz * yy[7])
    gy = R3 * yy[2] + uy * (s2 * yy[5] - h2 * yy[4]) + h2 * (ux * yy[6] + uz * yy[8])
    gz = R3 * yy[3] - 2.0 * s2 * uz * yy[5] + h2 * (ux * yy[7] + uy * yy[8])
    along = ux * gx + uy * gy + uz * gz
    zero = jnp.zeros((5, EDGES), F32)
    disp = jnp.concatenate(
        [
            live * ((gx - ux * along) * inv + ux * d_r),
            live * ((gy - uy * along) * inv + uy * d_r),
            live * ((gz - uz * along) * inv + uz * d_r),
            zero,
        ],
        0,
    )
    hi, mid, lo = pieces(disp)
    disp24 = jnp.concatenate([hi, mid, lo], 0).astype(BF16)
    acc = None
    mine = None
    for k in range(8):
        term = disp[:, k * 128 : (k + 1) * 128]
        mine = term if mine is None else mine + term
    own[...] = slot_total(mine)
    for i in range(4):
        cols = pl.ds(i * 256, 256)
        hot = jnp.where(iota((NTAB, 256), 0) == slots[:, cols], 1.0, 0.0).astype(BF16)
        term = dot(disp24[:, i * 256 : (i + 1) * 256], hot, 1, 1)
        acc = term if acc is None else acc + term
    ghost[...] = acc[0:8] + acc[8:16] + acc[16:24]

    edge_energy = smooth * lat_out
    total = None
    for k in range(8):
        term = edge_energy[:, k * 128 : (k + 1) * 128]
        total = term if total is None else total + term
    total = slot_total(jnp.broadcast_to(total, (8, 128)))[0:1]
    hot = jnp.where(iota((NSPEC, 128), 0).astype(F32) == cent[3:4, 0:128], 1.0, 0.0)
    energy[...] = jnp.broadcast_to(
        jnp.sum(hot * scale[...], 0, keepdims=True) * total
        + jnp.sum(hot * shift[...], 0, keepdims=True),
        energy.shape,
    )
    cot = cent[4:5, 0:128] * jnp.where(iota((1, 128), 1) < ATOMS, 1.0, 0.0)
    stack = jnp.concatenate(
        [dpath[...], hot * (cot * total), hot * cot, jnp.zeros((64, 128), F32)], 0
    )
    row = jnp.sum(stack.T, 0, keepdims=True)
    misc[...] = jnp.broadcast_to(
        jnp.concatenate([row, jnp.zeros((1, 256), F32)], 1), misc.shape
    )


VSPEC = pl.BlockSpec(memory_space=pltpu.VMEM)
SSPEC = pl.BlockSpec(memory_space=pltpu.SMEM)


def call(body, outs, args, scratch=(), scalar=False, flops=0, limit=24):
    specs = [VSPEC] * len(args)
    if scalar:
        specs[0] = SSPEC
    return pl.pallas_call(
        body,
        out_shape=[pltpu.VMEM(shape, dtype) for shape, dtype in outs],
        in_specs=specs,
        out_specs=[VSPEC] * len(outs),
        scratch_shapes=[pltpu.VMEM(shape, dtype) for shape, dtype in scratch],
        compiler_params=pltpu.CompilerParams(vmem_limit_bytes=limit << 20),
        cost_estimate=pl.CostEstimate(flops=flops, bytes_accessed=1 << 20, transcendentals=0),
    )(*args)


def split_outside(x):
    hi = lax.reduce_precision(x, 8, 7)
    return hi.astype(BF16), (x - hi).astype(BF16)


def swap(x, axis, bit):
    count = lax.axis_size(axis)
    return lax.ppermute(x, axis, [(i, i ^ bit) for i in range(count)])


def is_up(axis, bit):
    return (lax.axis_index(axis) // bit) % 2


def halve(x, axis, bit, dim):
    size = x.shape[dim] // 2
    up = is_up(axis, bit)
    send = lax.dynamic_slice_in_dim(x, (1 - up) * size, size, dim)
    keep = lax.dynamic_slice_in_dim(x, up * size, size, dim)
    return keep + swap(send, axis, bit)


def unhalve(x, axis, bit, dim):
    other = swap(x, axis, bit)
    first = is_up(axis, bit) == 0
    return jnp.concatenate(
        [jnp.where(first, x, other), jnp.where(first, other, x)], axis=dim
    )


def bits_of(axis):
    bit = 1
    while bit < lax.axis_size(axis):
        yield bit
        bit *= 2


def plan(order, dims):
    steps = []
    rest = [("gx", b) for b in bits_of("gx")]
    if order:
        rest = rest[::-1]
    rest += [("gy", b) for b in bits_of("gy")] + [("gz", b) for b in bits_of("gz") if b > 1]
    for n, (axis, bit) in enumerate(rest):
        steps.append((axis, bit, dims[n] if n < len(dims) else None))
    return steps


def all_sum(piece, steps):
    for axis, bit, dim in steps:
        if dim is None:
            piece = piece + swap(piece, axis, bit)
        else:
            piece = halve(piece, axis, bit, dim)
    for axis, bit, dim in steps[::-1]:
        if dim is not None:
            piece = unhalve(piece, axis, bit, dim)
    return piece


def shifted(value, axis, by):
    length = lax.axis_size(axis)
    pairs = [(i, i + by) for i in range(length) if 0 <= i + by < length]
    return lax.ppermute(value, axis, pairs)


def with_halo(cells, sides):
    for axis, dim in sides:
        cells = jnp.concatenate(
            [shifted(cells, axis, 1), cells, shifted(cells, axis, -1)], axis=dim
        )
    return cells


def fold(ghost_grad, axis, dim):
    def part(i):
        return lax.slice_in_dim(ghost_grad, i, i + 1, axis=dim)

    return part(1) + shifted(part(2), axis, 1) + shifted(part(0), axis, -1)


def per_device(
    positions,
    species,
    neighbours,
    embed_center,
    embed_neigh,
    embed_radial,
    value_proj,
    env_weight,
    latent_weight,
    path_weight,
    out_weight,
    scale_table,
    shift_table,
    cotangent,
):
    core = is_up("gz", 1).astype(jnp.int32).reshape(1)
    carried = jnp.concatenate(
        [positions, species.astype(F32)[None], jnp.zeros((4, ATOMS), F32)], 0
    )
    table = with_halo(
        carried.reshape(8, 1, 1, 1, ATOMS), (("gz", 3), ("gy", 2), ("gx", 1))
    ).reshape(8, NTAB)
    own_rows = jnp.concatenate(
        [positions, species.astype(F32)[None], cotangent[None], jnp.zeros((3, ATOMS), F32)], 0
    )
    cent = jnp.tile(own_rows, (1, NB))
    slots = neighbours.reshape(1, EDGES)
    w0h, w0l = split_outside(latent_weight[0])
    w1h, w1l = split_outside(latent_weight[1])
    ve = jnp.concatenate([value_proj, env_weight[0]], 1)
    ev = env_weight[1]
    path = jnp.broadcast_to(path_weight.reshape(9 * CHANNELS, 1), (9 * CHANNELS, 128))
    outw = out_weight[:, None]
    scale = scale_table[:, None]
    shift = shift_table[:, None]

    big = 2 * EDGES * LATENT * WIDE * 3
    wide = ((WIDE, EDGES), BF16)
    half = ((HALF, EDGES), BF16)
    quarter = ((WIDE, QUARTER), F32)
    x0h, x0l, x1h, x1l, z0, pre, vw, w1, geo, g0, g1, f1 = call(
        fwd_kernel,
        [
            wide, wide, wide, wide,
            ((LATENT, EDGES), F32), ((LATENT, EDGES), F32), ((128, EDGES), F32),
            ((64, EDGES), F32), ((G_ROWS, EDGES), F32), ((576, 128), F32), ((576, 128), F32),
            ((576, EDGES), F32),
        ],
        (table, slots, cent, w0h, w0l, embed_center, embed_neigh, embed_radial, ve, ev, path,
         scale),
        [
            ((8, EDGES), F32), ((288, LATENT), BF16), ((LATENT, 128), BF16), ((LATENT, 128), BF16),
            ((LATENT, 64), BF16), ((LATENT, 64), BF16),
        ],
        flops=3 * big,
    )

    late = []
    for h in range(2):
        late.append(
            call(
                functools.partial(late_kernel, h),
                [half, half, quarter, quarter, ((8, EDGES), F32), ((8, HALF), F32)],
                (core, x1h, x1l, w1h, w1l, outw, geo),
                [((HALF, 128), F32)],
                scalar=True,
                flops=big,
            )
        )
    (qah, qal, keep_a, send_a, sla, outa), (qbh, qbl, keep_b, send_b, slb, outb) = late
    lat_a = all_sum(keep_a + swap(send_a, "gz", 1), plan(0, (0, 0, 0, 1)))
    lat_b = all_sum(keep_b + swap(send_b, "gz", 1), plan(1, (0, 0, 0, 1)))

    ds1, dw1h, dw1l, dy1 = call(
        mid_kernel,
        [((192, EDGES), F32), ((64, EDGES), BF16), ((64, EDGES), BF16), ((16, EDGES), F32)],
        (qah, qal, qbh, qbl, w1h, w1l, f1, g1, w1, geo),
        [((576, 128), F32)],
        flops=big // 4,
    )
    early = []
    for h in range(2):
        early.append(
            call(
                functools.partial(early_kernel, h),
                [((HALF, EDGES), F32), half, half, quarter, quarter, ((8, EDGES), F32)],
                (core, qah, qal, qbh, qbl, w1h, w1l, ev, dw1h, dw1l, outw, geo, z0, x0h, x0l),
                [((HALF, 64), BF16), ((HALF, 64), BF16)],
                scalar=True,
                flops=big,
            )
        )
    (dla, rah, ral, keep_c, send_c, sea), (dlb, rbh, rbl, keep_d, send_d, seb) = early
    lat_c = all_sum(keep_c + swap(send_c, "gz", 1), plan(0, (0, 0, 0, 1)))
    lat_d = all_sum(keep_d + swap(send_d, "gz", 1), plan(1, (0, 0, 0, 1)))

    dvwh, dvwl, dy, dpath, dve, dev = call(
        couple_kernel,
        [
            ((128, EDGES), BF16), ((128, EDGES), BF16), ((16, EDGES), F32), ((576, 128), F32),
            ((128, LATENT), F32), ((64, LATENT), F32),
        ],
        (rah, ral, rbh, rbl, w0h, w0l, vw, geo, g0, g1, ds1, path, x0h, x0l, x1h, x1l, dw1h, dw1l,
         dy1),
        [((192, EDGES), F32), ((576, 128), F32), ((16, EDGES), F32)],
        flops=big // 3,
    )
    hots_grad, rad_grad, ghost, own, energy, misc = call(
        last_kernel,
        [
            ((128, LATENT), F32), ((8, LATENT), F32), ((8, NTAB), F32), ((8, 128), F32),
            ((8, 128), F32), ((8, LATENT), F32),
        ],
        (rah, ral, rbh, rbl, w0h, w0l, ve, dvwh, dvwl, dla, dlb, pre, geo, slots, cent,
         embed_radial, sla, slb, sea, seb, dy, dpath, scale, shift),
        [
            ((LATENT, 128), BF16), ((LATENT, 128), BF16), ((LATENT, EDGES), BF16),
            ((LATENT, EDGES), BF16), ((1, EDGES), F32), ((8, EDGES), F32),
        ],
        flops=2 * big,
    )
    dout = jnp.concatenate([outa, outb], 1)
    small = jnp.concatenate([hots_grad, dve, dev, rad_grad, misc[0:1], dout[0:1], misc[2:8]], 0)
    small = halve(small, "gz", 1, 1)
    small = all_sum(small, plan(0, (0, 1, 1)))
    small = unhalve(small, "gz", 1, 1)
    misc_row = small[328]

    ghost_grad = ghost[0:3].reshape(3, 3, 3, 3, ATOMS)
    ghost_grad = fold(fold(fold(ghost_grad, "gx", 1), "gy", 2), "gz", 3)
    position_grad = ghost_grad.reshape(3, ATOMS) - own[0:3, 0:ATOMS]

    first = is_up("gz", 1) == 0

    def joined(mine):
        other = swap(mine, "gz", 1)
        return [jnp.where(first, mine, other), jnp.where(first, other, mine)]

    d_latent = jnp.stack(
        [
            jnp.concatenate(joined(lat_c) + joined(lat_d), 1),
            jnp.concatenate(joined(lat_a) + joined(lat_b), 1),
        ]
    )
    return (
        energy[0, 0:ATOMS],
        position_grad,
        small[0:64],
        small[64:128],
        small[320:328],
        small[128:192].T,
        jnp.stack([small[192:256].T, small[256:320].T]),
        d_latent,
        misc_row[0:576].reshape(9, CHANNELS),
        small[329],
        misc_row[576:640],
        misc_row[640:704],
    )


def solution(mesh):
    everything = ("gx", "gy", "gz")
    return jax.shard_map(
        per_device,
        mesh=mesh,
        in_specs=(
            P(None, everything),
            P(everything),
            P(None, everything),
            P(),
            P(),
            P(),
            P(),
            P(),
            P(),
            P(),
            P(),
            P(),
            P(),
            P(everything),
        ),
        out_specs=(
            P(everything),
            P(None, everything),
            P(),
            P(),
            P(),
            P(),
            P(),
            P(),
            P(),
            P(),
            P(),
            P(),
        ),
        check_vma=False,
    )
```

time: 654 us -> 375 us (0.57)
  matrix products: 250 us -> 0 us
  Pallas kernels: 0 us -> 89.7 us
  other arithmetic: 84.8 us -> 34.7 us
  starting transfers between devices: 33.5 us -> 82.1 us
  blocking collectives: 41.9 us -> 0 us
  waiting for transfers between devices: 138 us -> 102 us
  local copies, waits for them, and re-layouts: 83.1 us -> 59.4 us
  between operations: 16.9 us -> 2.3 us
    dot_general x34 -> x0, matrix products: 250 us -> none  [the longest x28 219 us: product(): jnp.dot(left_side, right_side, precision=PRECISE, preferred_element_type=...]
    psum x1 -> x0, waiting for transfers between devices: 132 us -> none  [per_device(): lax.psum((d_env_early, d_lat_early, d_path, d_center, d_neigh, d_radial,...]
    ppermute x6 -> x49, waiting for transfers between devices: 1.2 us -> 98.7 us  [swap(): return lax.ppermute(x, axis, [(i, i ^ bit) for i in range(count)])]
    pallas_call x0 -> x8, Pallas kernels: none -> 89.7 us  [call(): pl.pallas_call(body, out_shape=[pltpu.VMEM(shape, dtype) for shape, dtype...]
    psum x1 -> x0, blocking collectives: 41.9 us -> none  [per_device(): lax.psum((d_env_early, d_lat_early, d_path, d_center, d_neigh, d_radial,...]
    ppermute x6 -> x49, starting transfers between devices: 17.1 us -> 48.2 us  [swap(): return lax.ppermute(x, axis, [(i, i ^ bit) for i in range(count)])]
    reduce_sum x17 -> x0, other arithmetic: 30.3 us -> none  [the longest x2 6.58 us: environment(): jnp.broadcast_to(summed[:, :, None, :], (9, CHANNELS, NB, atom_count))]
    unnamed x393 -> x139, local copies, waits for them, and re-layouts: 12.9 us -> 39.8 us
  transfers between devices with their start and end apart: 13 -> 61, of which waited for: 4 -> 31; matrix products, arithmetic and copies ran while one was open for 7% -> 10% of each run, Pallas kernels for 0% -> 0%
where the time goes in v1:
time: 375 us; the launch traced here: 370 us
  waiting for transfers between devices  102 us (27%)
  Pallas kernels  89.7 us (24%)
  starting transfers between devices  82.1 us (22%)
  local copies, waits for them, and re-layouts  59.4 us (16%)
  other arithmetic  34.7 us (9%)
    ppermute x49, waiting for transfers between devices, swap(): return lax.ppermute(x, axis, [(i, i ^ bit) for i in range(count)])  98.7 us
    pallas_call x8, Pallas kernels, call(): pl.pallas_call(body, out_shape=[pltpu.VMEM(shape, dtype) for shape, dtype...  89.7 us
    ppermute x49, starting transfers between devices, swap(): return lax.ppermute(x, axis, [(i, i ^ bit) for i in range(count)])  48.2 us
    unnamed x139, local copies, waits for them, and re-layouts  39.8 us
    ppermute x12, starting transfers between devices, shifted(): return lax.ppermute(value, axis, pairs)  33.9 us
  transfers between devices with their start and end apart: 61, of which 31 were waited for; matrix products, arithmetic and copies ran while one was open for 10% of the time, Pallas kernels for 0%

profile of v1, /device:TPU:0, one launch (start us, length us, event | category | flops | bytes accessed | tf_op | source)
XLA Modules:
  0.0 370.4 jit_solution(12414350282391998233)
XLA Ops:
  4.2 3.0 collective-permute-start
  7.3 7.0 %fusion.1 = (bf16[1216,1024]{1,0:T(8,128)(2,1)S(1)}, bf16[1216,1024]{1,0:T(8,128)(2,1)}, bf16[1216,1024]{1,0:T(8,128)(2,1)}, bf16[1216,1024]{1,0:T(8,128)(2,1)}) fusion(f32[2,1216,1024]{2,1,0:T(8,128)} %param.22), kind=kLoop, calls=%fused_computation.6 | loop fusion | flops 9961472 | bytes 19922944 | tf_op jit(solution)/shard_map/convert_element_type | solution.py:665
  16.2 6.2 %collective-permute-start.2 = (f32[8,1,1,3,32]{4,3,2,1,0:T(4,128)}, f32[8,1,1,3,32]{4,3,2,1,0:T(4,128)}, u32[]{:S(2)}, u32[]{:S(2)}) collective-permute-start(f32[8,1,1,3,32]{4,3,2,1,0:T(4,128)} %pad_maximum_fusion.24), channel_id=1, source_target_pairs={{0,2},{2,4},{4,6},{1,3},{3,5},{5,7},{8,10},{10,12},{12,14},{9,11},... | collective-permute-start | bytes 9224 | tf_op jit(solution)/shard_map/ppermute | solution.py:726
  27.0 5.2 %collective-permute-start.4 = (f32[8,1,3,3,32]{4,3,2,1,0:T(4,128)}, f32[8,1,3,3,32]{4,3,2,1,0:T(4,128)}, u32[]{:S(2)}, u32[]{:S(2)}) collective-permute-start(f32[8,1,3,3,32]{4,3,2,1,0:T(4,128)} %pad_maximum_fusion.23), channel_id=1, source_target_pairs={{0,8},{8,16},{16,24},{1,9},{9,17},{17,25},{2,10},{10,18},{18,26},{... | collective-permute-start | bytes 27656 | tf_op jit(solution)/shard_map/ppermute | solution.py:726
  39.6 1.7 copy.39.outw
  42.6 1.6 pad_maximum_fusion.22
  44.2 1.6 reshape.57.tab
  46.7 1.7 copy-done.1
  48.4 1.7 copy-done.3
  55.0 21.7 %shard_map.229 = (bf16[1216,1024]{1,0:T(8,128)(2,1)S(1)}, bf16[1216,1024]{1,0:T(8,128)(2,1)S(1)}, bf16[1216,1024]{1,0:T(8,128)(2,1)S(1)}, bf16[1216,1024]{1,0:T(...) custom-call(f32[8,864]{1,0:T(8,128)S(1)} %copy-done.44, ...), custom_call_target="tpu_custom_call" | custom-call | flops 22951231488 | bytes 1048576 | tf_op jit(solution)/shard_map/pallas_call | solution.py:652
  78.2 2.0 copy-done.57
  80.2 2.1 copy-done.63
  82.3 3.6 copy-done.10
  85.9 10.6 %shard_map.230 = (bf16[512,1024]{1,0:T(8,128)(2,1)S(1)}, bf16[512,1024]{1,0:T(8,128)(2,1)S(1)}, f32[1216,256]{1,0:T(8,128)S(1)}, f32[1216,256]{1,0:T(8,128)S(1)}...) custom-call(s32[1]{0:T(128)} %bitcast.core, bf16[1216,1024]{1,0:T(8,128)(2,1)S(1)} %get-tuple-element.64.x1h, ...), custom_call_target="tpu_custom_call" | custom-call | flops 7650410496 | bytes 1048576 | tf_op jit(solution)/shard_map/pallas_call | solution.py:652
  98.6 10.8 %shard_map.231 = (bf16[512,1024]{1,0:T(8,128)(2,1)S(1)}, bf16[512,1024]{1,0:T(8,128)(2,1)S(1)}, f32[1216,256]{1,0:T(8,128)S(1)}, f32[1216,256]{1,0:T(8,128)S(1)}...) custom-call(s32[1]{0:T(128)} %bitcast.core, bf16[1216,1024]{1,0:T(8,128)(2,1)S(1)} %get-tuple-element.64.x1h, ...), custom_call_target="tpu_custom_call" | custom-call | flops 7650410496 | bytes 1048576 | tf_op jit(solution)/shard_map/pallas_call | solution.py:652
  111.6 2.7 shard_map.232
  115.3 9.6 %shard_map.233 = (f32[512,1024]{1,0:T(8,128)S(1)}, bf16[512,1024]{1,0:T(8,128)(2,1)S(1)}, bf16[512,1024]{1,0:T(8,128)(2,1)S(1)}, f32[1216,256]{1,0:T(8,128)S(1)}...) custom-call(s32[1]{0:T(128)} %bitcast.core, bf16[512,1024]{1,0:T(8,128)(2,1)S(1)} %get-tuple-element.67.qah, ...), custom_call_target="tpu_custom_call" | custom-call | flops 7650410496 | bytes 1048576 | tf_op jit(solution)/shard_map/pallas_call | solution.py:652
  128.3 1.7 copy-done.6
  130.9 10.0 %shard_map.234 = (f32[512,1024]{1,0:T(8,128)S(1)}, bf16[512,1024]{1,0:T(8,128)(2,1)S(1)}, bf16[512,1024]{1,0:T(8,128)(2,1)S(1)}, f32[1216,256]{1,0:T(8,128)S(1)}...) custom-call(s32[1]{0:T(128)} %bitcast.core, bf16[512,1024]{1,0:T(8,128)(2,1)S(1)} %get-tuple-element.67.qah, ...), custom_call_target="tpu_custom_call" | custom-call | flops 7650410496 | bytes 1048576 | tf_op jit(solution)/shard_map/pallas_call | solution.py:652
  142.3 1.7 copy-done.25
  145.2 10.1 %shard_map.235 = (bf16[128,1024]{1,0:T(8,128)(2,1)S(1)}, bf16[128,1024]{1,0:T(8,128)(2,1)S(1)}, f32[16,1024]{1,0:T(8,128)S(1)}, f32[576,128]{1,0:T(8,128)S(1)}, ...) custom-call(bf16[512,1024]{1,0:T(8,128)(2,1)S(1)} %get-tuple-element.79.qah, ...), custom_call_target="tpu_custom_call" | custom-call | flops 2550136832 | bytes 1048576 | tf_op jit(solution)/shard_map/pallas_call | solution.py:652
  157.8 2.2 copy-done.64
  160.0 14.2 %shard_map.236 = (f32[128,1024]{1,0:T(8,128)S(1)}, f32[8,1024]{1,0:T(8,128)S(1)}, f32[8,864]{1,0:T(8,128)S(1)}, f32[8,128]{1,0:T(8,128)S(1)}, f32[8,128]{1,0:T(8,128)S(1)}, /*index=5*/f32[8,1024]{1,0:T(8,128)S(1)}) custom-call(bf16[512,1024]{1,0:T(8,128)(2,1)S(1)} %get-tuple-element.79.qah, bf16[512,1024]{1,0:T(8,128)(2,1)S(1)} %get-tuple-element.80.qal, ...), custom_call_target="tpu_custom_call" | custom-call | flops 15300820992 | bytes 1048576 | tf_op jit(solution)/shard_map/pallas_call | solution.py:652
  174.2 3.7 concatenate.97
  177.9 2.1 constant_dynamic-slice_fusion.19
  181.4 4.7 %collective-permute-start.6 = (f32[3,1,3,3,32]{4,0,3,2,1:T(4,128)S(1)}, f32[3,1,3,3,32]{4,0,3,2,1:T(4,128)S(1)}, u32[]{:S(2)}, u32[]{:S(2)}) collective-permute-start(f32[3,1,3,3,32]{4,0,3,2,1:T(4,128)S(1)} %copy.51), channel_id=1, source_target_pairs={{0,8},{8,16},{16,24},{1,9},{9,17},{17,25},{2,10},{10,18},{18,26},{... | collective-permute-start | bytes 10376 | tf_op jit(solution)/shard_map/ppermute | solution.py:726
  189.0 4.7 %collective-permute-start.8 = (f32[3,1,1,3,32]{4,0,3,2,1:T(4,128)S(1)}, f32[3,1,1,3,32]{4,0,3,2,1:T(4,128)S(1)}, u32[]{:S(2)}, u32[]{:S(2)}) collective-permute-start(f32[3,1,1,3,32]{4,0,3,2,1:T(4,128)S(1)} %get-tuple-element.180), channel_id=1, source_target_pairs={{0,2},{2,4},{4,6},{1,3},{3,5},{5,7},{8,10},{10,12},{12,14},{9,11},... | collective-permute-start | bytes 3464 | tf_op jit(solution)/shard_map/ppermute | solution.py:726
  195.0 3.0 collective-permute-start.13
  199.5 5.5 %collective-permute-done.13 = f32[168,512]{1,0:T(8,128)S(1)} collective-permute-done((f32[168,512]{1,0:T(8,128)S(1)}, f32[168,512]{1,0:T(8,128)S(1)}, u32[]{:S(2)}, u32[]{:S(2)}) %collective-permute-start.13) | collective-permute-done | bytes 344096 | tf_op jit(solution)/shard_map/ppermute | solution.py:670
  205.1 3.2 collective-permute-start.14
  208.3 3.4 collective-permute-done.14
  213.0 1.7 collective-permute-done.11
  214.7 2.2 collective-permute-start.10
  219.9 2.5 collective-permute-done.15
  222.4 2.7 collective-permute-start.16
  225.1 2.1 collective-permute-start.32
  227.4 1.8 collective-permute-done.16
  230.4 3.4 collective-permute-done.17
  233.8 2.1 collective-permute-start.18
  236.9 8.9 %collective-permute-done.18 = f32[168,256]{1,0:T(8,128)S(1)} collective-permute-done((f32[168,256]{1,0:T(8,128)S(1)}, f32[168,256]{1,0:T(8,128)S(1)}, u32[]{:S(2)}, u32[]{:S(2)}) %collective-permute-start.18) | collective-permute-done | bytes 172064 | tf_op jit(solution)/shard_map/ppermute | solution.py:670
  248.3 2.1 collective-permute-start.23
  250.4 8.8 %collective-permute-done.52 = f32[608,256]{1,0:T(8,128)S(1)} collective-permute-done((f32[608,256]{1,0:T(8,128)S(1)}, f32[608,256]{1,0:T(8,128)S(1)}, u32[]{:S(2)}, u32[]{:S(2)}) %collective-permute-start.52) | collective-permute-done | bytes 622624 | tf_op jit(solution)/shard_map/ppermute | solution.py:670
  260.1 2.1 collective-permute-start.43
  262.2 5.2 %collective-permute-done.19 = f32[168,512]{1,0:T(8,128)S(1)} collective-permute-done((f32[168,512]{1,0:T(8,128)S(1)}, f32[168,512]{1,0:T(8,128)S(1)}, u32[]{:S(2)}, u32[]{:S(2)}) %collective-permute-start.19) | collective-permute-done | bytes 344096 | tf_op jit(solution)/shard_map/ppermute | solution.py:670
  267.5 6.5 %collective-permute-done.33 = f32[304,256]{1,0:T(8,128)S(1)} collective-permute-done((f32[304,256]{1,0:T(8,128)S(1)}, f32[304,256]{1,0:T(8,128)S(1)}, u32[]{:S(2)}, u32[]{:S(2)}) %collective-permute-start.33) | collective-permute-done | bytes 311328 | tf_op jit(solution)/shard_map/ppermute | solution.py:670
  280.0 2.7 collective-permute-done.34
  283.1 3.4 collective-permute-done.24
  286.6 2.6 collective-permute-done.54
  290.1 2.2 collective-permute-done.44
  292.6 2.8 collective-permute-start.36
  295.4 4.2 %collective-permute-done.25 = f32[152,128]{1,0:T(8,128)S(1)} collective-permute-done((f32[152,128]{1,0:T(8,128)S(1)}, f32[152,128]{1,0:T(8,128)S(1)}, u32[]{:S(2)}, u32[]{:S(2)}) %collective-permute-start.25) | collective-permute-done | bytes 77856 | tf_op jit(solution)/shard_map/ppermute | solution.py:670
  299.7 1.6 collective-permute-done.55
  304.3 2.0 collective-permute-done.36
  311.7 2.3 collective-permute-done.37
  315.3 2.0 collective-permute-done.27
  318.1 2.0 collective-permute-start.28
  322.3 2.0 collective-permute-start.48
  332.6 1.8 collective-permute-start.59
  336.4 11.1 %collective-permute-done.39 = f32[608,256]{1,0:T(8,128)S(1)} collective-permute-done((f32[608,256]{1,0:T(8,128)S(1)}, f32[608,256]{1,0:T(8,128)S(1)}, u32[]{:S(2)}, u32[]{:S(2)}) %collective-permute-start.39) | collective-permute-done | bytes 622624 | tf_op jit(solution)/shard_map/ppermute | solution.py:670
  348.5 10.1 %collective-permute-done.59 = f32[608,256]{1,0:T(8,128)S(1)} collective-permute-done((f32[608,256]{1,0:T(8,128)S(1)}, f32[608,256]{1,0:T(8,128)S(1)}, u32[]{:S(2)}, u32[]{:S(2)}) %collective-permute-start.59) | collective-permute-done | bytes 622624 | tf_op jit(solution)/shard_map/ppermute | solution.py:670
  359.9 1.8 collective-permute-done.60
  361.9 1.6 collective-permute-done.50
  363.7 1.6 maximum_bitcast_fusion
  365.3 5.0 %pad_maximum_fusion = f32[2,1216,1024]{2,1,0:T(8,128)} fusion(f32[1,1216,1024]{2,1,0:T(8,128)S(1)} %get-tuple-element.187, f32[1,1216,1024]{2,1,0:T(8,128)S(1)} %get-tuple-element.186), kind=kLoop, calls=%fused_computation | loop fusion | flops 2490368 | bytes 19922944 | tf_op jit(solution)/shard_map/stack | solution.py:883
  (336 shorter events, 90.6 us)
Async XLA Ops:
  2.8 11.4 %collective-permute-start.1 = (f32[8,1,1,1,32]{4,3,2,1,0:T(1,128)S(1)}, f32[8,1,1,1,32]{4,3,2,1,0:T(1,128)S(1)}, u32[]{:S(2)}, u32[]{:S(2)}) collective-permute-start(f32[8,1,1,1,32]{4,3,2,1,0:T(1,128)S(1)} %bitcast.45), channel_id=1, source_target_pairs={{1,0},{3,2},{5,4},{7,6},{9,8},{11,10},{13,12},{15,14},{17,16},{19,... | collective-permute-start | bytes 3080 | tf_op jit(solution)/shard_map/ppermute | solution.py:726
  4.2 10.0 %collective-permute-start = (f32[8,1,1,1,32]{4,3,2,1,0:T(1,128)S(1)}, f32[8,1,1,1,32]{4,3,2,1,0:T(1,128)S(1)}, u32[]{:S(2)}, u32[]{:S(2)}) collective-permute-start(f32[8,1,1,1,32]{4,3,2,1,0:T(1,128)S(1)} %bitcast.46), channel_id=1, source_target_pairs={{0,1},{2,3},{4,5},{6,7},{8,9},{10,11},{12,13},{14,15},{16,17},{18,... | collective-permute-start | bytes 3080 | tf_op jit(solution)/shard_map/ppermute | solution.py:726
  14.9 9.4 %collective-permute-start.3 = (f32[8,1,1,3,32]{4,3,2,1,0:T(4,128)}, f32[8,1,1,3,32]{4,3,2,1,0:T(4,128)}, u32[]{:S(2)}, u32[]{:S(2)}) collective-permute-start(f32[8,1,1,3,32]{4,3,2,1,0:T(4,128)} %pad_maximum_fusion.24), channel_id=1, source_target_pairs={{2,0},{4,2},{6,4},{3,1},{5,3},{7,5},{10,8},{12,10},{14,12},{11,9},... | collective-permute-start | bytes 9224 | tf_op jit(solution)/shard_map/ppermute | solution.py:726
  16.2 8.1 %collective-permute-start.2 = (f32[8,1,1,3,32]{4,3,2,1,0:T(4,128)}, f32[8,1,1,3,32]{4,3,2,1,0:T(4,128)}, u32[]{:S(2)}, u32[]{:S(2)}) collective-permute-start(f32[8,1,1,3,32]{4,3,2,1,0:T(4,128)} %pad_maximum_fusion.24), channel_id=1, source_target_pairs={{0,2},{2,4},{4,6},{1,3},{3,5},{5,7},{8,10},{10,12},{12,14},{9,11},... | collective-permute-start | bytes 9224 | tf_op jit(solution)/shard_map/ppermute | solution.py:726
  25.7 17.0 %collective-permute-start.5 = (f32[8,1,3,3,32]{4,3,2,1,0:T(4,128)}, f32[8,1,3,3,32]{4,3,2,1,0:T(4,128)}, u32[]{:S(2)}, u32[]{:S(2)}) collective-permute-start(f32[8,1,3,3,32]{4,3,2,1,0:T(4,128)} %pad_maximum_fusion.23), channel_id=1, source_target_pairs={{8,0},{16,8},{24,16},{9,1},{17,9},{25,17},{10,2},{18,10},{26,18},{... | collective-permute-start | bytes 27656 | tf_op jit(solution)/shard_map/ppermute | solution.py:726
  27.0 15.7 %collective-permute-start.4 = (f32[8,1,3,3,32]{4,3,2,1,0:T(4,128)}, f32[8,1,3,3,32]{4,3,2,1,0:T(4,128)}, u32[]{:S(2)}, u32[]{:S(2)}) collective-permute-start(f32[8,1,3,3,32]{4,3,2,1,0:T(4,128)} %pad_maximum_fusion.23), channel_id=1, source_target_pairs={{0,8},{8,16},{16,24},{1,9},{9,17},{17,25},{2,10},{10,18},{18,26},{... | collective-permute-start | bytes 27656 | tf_op jit(solution)/shard_map/ppermute | solution.py:726
  36.8 39.9 %copy-start.33 = (f32[1,1024,64]{2,1,0:T(8,128)}, f32[1,1024,64]{2,1,0:T(8,128)S(1)}, u32[]{:S(2)}) copy-start(f32[1,1024,64]{2,1,0:T(8,128)S(1)} %copy.49) | copy-start | bytes 786436
  82.2 33.0 %copy-start.5 = (bf16[1216,1024]{1,0:T(8,128)(2,1)}, bf16[1216,1024]{1,0:T(8,128)(2,1)S(1)}, u32[]{:S(2)}) copy-start(bf16[1216,1024]{1,0:T(8,128)(2,1)S(1)} %get-tuple-element.78.x0l) | copy-start | bytes 7471108
  82.2 33.0 %copy-start.26 = (f32[32,1024]{1,0:T(8,128)}, f32[32,1024]{1,0:T(8,128)S(1)}, u32[]{:S(2)}) copy-start(f32[32,1024]{1,0:T(8,128)S(1)} %get-tuple-element.66.geo) | copy-start | bytes 393220
  180.0 13.7 %collective-permute-start.12 = (f32[336,512]{1,0:T(8,128)}, f32[336,512]{1,0:T(8,128)S(1)}, u32[]{:S(2)}, u32[]{:S(2)}) collective-permute-start(f32[336,512]{1,0:T(8,128)} %constant_dynamic-slice_fusion.19), channel_id=1, source_target_pairs={{0,1},{1,0},{2,3},{3,2},{4,5},{5,4},{6,7},{7,6},{8,9},{9,8},{10,11... | collective-permute-start | bytes 2064392 | tf_op jit(solution)/shard_map/ppermute | solution.py:670
  180.1 6.2 %collective-permute-start.7 = (f32[3,1,3,3,32]{4,0,3,2,1:T(4,128)S(1)}, f32[3,1,3,3,32]{4,0,3,2,1:T(4,128)S(1)}, u32[]{:S(2)}, u32[]{:S(2)}) collective-permute-start(f32[3,1,3,3,32]{4,0,3,2,1:T(4,128)S(1)} %copy.52), channel_id=1, source_target_pairs={{8,0},{16,8},{24,16},{9,1},{17,9},{25,17},{10,2},{18,10},{26,18},{... | collective-permute-start | bytes 10376 | tf_op jit(solution)/shard_map/ppermute | solution.py:726
  181.4 6.2 %collective-permute-start.6 = (f32[3,1,3,3,32]{4,0,3,2,1:T(4,128)S(1)}, f32[3,1,3,3,32]{4,0,3,2,1:T(4,128)S(1)}, u32[]{:S(2)}, u32[]{:S(2)}) collective-permute-start(f32[3,1,3,3,32]{4,0,3,2,1:T(4,128)S(1)} %copy.51), channel_id=1, source_target_pairs={{0,8},{8,16},{16,24},{1,9},{9,17},{17,25},{2,10},{10,18},{18,26},{... | collective-permute-start | bytes 10376 | tf_op jit(solution)/shard_map/ppermute | solution.py:726
  187.7 11.3 %collective-permute-start.9 = (f32[3,1,1,3,32]{4,0,3,2,1:T(4,128)S(1)}, f32[3,1,1,3,32]{4,0,3,2,1:T(4,128)S(1)}, u32[]{:S(2)}, u32[]{:S(2)}) collective-permute-start(f32[3,1,1,3,32]{4,0,3,2,1:T(4,128)S(1)} %get-tuple-element.181), channel_id=1, source_target_pairs={{2,0},{4,2},{6,4},{3,1},{5,3},{7,5},{10,8},{12,10},{14,12},{11,9},... | collective-permute-start | bytes 3464 | tf_op jit(solution)/shard_map/ppermute | solution.py:726
  189.0 10.1 %collective-permute-start.8 = (f32[3,1,1,3,32]{4,0,3,2,1:T(4,128)S(1)}, f32[3,1,1,3,32]{4,0,3,2,1:T(4,128)S(1)}, u32[]{:S(2)}, u32[]{:S(2)}) collective-permute-start(f32[3,1,1,3,32]{4,0,3,2,1:T(4,128)S(1)} %get-tuple-element.180), channel_id=1, source_target_pairs={{0,2},{2,4},{4,6},{1,3},{3,5},{5,7},{8,10},{10,12},{12,14},{9,11},... | collective-permute-start | bytes 3464 | tf_op jit(solution)/shard_map/ppermute | solution.py:726
  195.0 10.0 %collective-permute-start.13 = (f32[168,512]{1,0:T(8,128)S(1)}, f32[168,512]{1,0:T(8,128)S(1)}, u32[]{:S(2)}, u32[]{:S(2)}) collective-permute-start(f32[168,512]{1,0:T(8,128)S(1)} %constant_dynamic-slice_fusion.18), channel_id=1, source_target_pairs={{0,8},{8,0},{16,24},{24,16},{1,9},{9,1},{17,25},{25,17},{2,10},{10... | collective-permute-start | bytes 1032200 | tf_op jit(solution)/shard_map/ppermute | solution.py:670
  198.5 21.2 %collective-permute-start.31 = (f32[1216,256]{1,0:T(8,128)S(1)}, f32[1216,256]{1,0:T(8,128)S(1)}, u32[]{:S(2)}, u32[]{:S(2)}) collective-permute-start(f32[1216,256]{1,0:T(8,128)S(1)} %copy-done.52), channel_id=1, source_target_pairs={{0,1},{1,0},{2,3},{3,2},{4,5},{5,4},{6,7},{7,6},{8,9},{9,8},{10,11... | collective-permute-start | bytes 3735560 | tf_op jit(solution)/shard_map/ppermute | solution.py:670
  198.5 28.7 %collective-permute-start.21 = (f32[1216,256]{1,0:T(8,128)S(1)}, f32[1216,256]{1,0:T(8,128)S(1)}, u32[]{:S(2)}, u32[]{:S(2)}) collective-permute-start(f32[1216,256]{1,0:T(8,128)S(1)} %copy-done.50), channel_id=1, source_target_pairs={{0,1},{1,0},{2,3},{3,2},{4,5},{5,4},{6,7},{7,6},{8,9},{9,8},{10,11... | collective-permute-start | bytes 3735560 | tf_op jit(solution)/shard_map/ppermute | solution.py:670
  199.0 31.2 %collective-permute-start.51 = (f32[1216,256]{1,0:T(8,128)S(1)}, f32[1216,256]{1,0:T(8,128)S(1)}, u32[]{:S(2)}, u32[]{:S(2)}) collective-permute-start(f32[1216,256]{1,0:T(8,128)S(1)} %copy-done.48), channel_id=1, source_target_pairs={{0,1},{1,0},{2,3},{3,2},{4,5},{5,4},{6,7},{7,6},{8,9},{9,8},{10,11... | collective-permute-start | bytes 3735560 | tf_op jit(solution)/shard_map/ppermute | solution.py:670
  199.1 37.0 %collective-permute-start.41 = (f32[1216,256]{1,0:T(8,128)S(1)}, f32[1216,256]{1,0:T(8,128)S(1)}, u32[]{:S(2)}, u32[]{:S(2)}) collective-permute-start(f32[1216,256]{1,0:T(8,128)S(1)} %copy-done.46), channel_id=1, source_target_pairs={{0,1},{1,0},{2,3},{3,2},{4,5},{5,4},{6,7},{7,6},{8,9},{9,8},{10,11... | collective-permute-start | bytes 3735560 | tf_op jit(solution)/shard_map/ppermute | solution.py:670
  205.1 6.6 %collective-permute-start.14 = (f32[168,256]{1,0:T(8,128)S(1)}, f32[168,256]{1,0:T(8,128)S(1)}, u32[]{:S(2)}, u32[]{:S(2)}) collective-permute-start(f32[168,256]{1,0:T(8,128)S(1)} %constant_dynamic-slice_fusion.17), channel_id=1, source_target_pairs={{0,16},{8,24},{16,0},{24,8},{1,17},{9,25},{17,1},{25,9},{2,18},{10... | collective-permute-start | bytes 516104 | tf_op jit(solution)/shard_map/ppermute | solution.py:670
  211.7 3.0 collective-permute-start.11
  214.7 2.9 collective-permute-start.10
  217.6 4.8 %collective-permute-start.15 = (f32[168,128]{1,0:T(8,128)S(1)}, f32[168,128]{1,0:T(8,128)S(1)}, u32[]{:S(2)}, u32[]{:S(2)}) collective-permute-start(f32[168,128]{1,0:T(8,128)S(1)} %constant_dynamic-slice_fusion.16), channel_id=1, source_target_pairs={{0,2},{2,0},{4,6},{6,4},{1,3},{3,1},{5,7},{7,5},{8,10},{10,8},{12,... | collective-permute-start | bytes 258056 | tf_op jit(solution)/shard_map/ppermute | solution.py:670
  222.4 6.8 %collective-permute-start.16 = (f32[168,128]{1,0:T(8,128)S(1)}, f32[168,128]{1,0:T(8,128)S(1)}, u32[]{:S(2)}, u32[]{:S(2)}) collective-permute-start(f32[168,128]{1,0:T(8,128)S(1)} %dynamic-slice_add_fusion.15), channel_id=1, source_target_pairs={{0,4},{2,6},{4,0},{6,2},{1,5},{3,7},{5,1},{7,3},{8,12},{10,14},{12... | collective-permute-start | bytes 258056 | tf_op jit(solution)/shard_map/ppermute | solution.py:670
  225.1 21.4 %collective-permute-start.32 = (f32[608,256]{1,0:T(8,128)S(1)}, f32[608,256]{1,0:T(8,128)S(1)}, u32[]{:S(2)}, u32[]{:S(2)}) collective-permute-start(f32[608,256]{1,0:T(8,128)S(1)} %constant_dynamic-slice_fusion.11), channel_id=1, source_target_pairs={{0,16},{8,24},{16,0},{24,8},{1,17},{9,25},{17,1},{25,9},{2,18},{10... | collective-permute-start | bytes 1867784 | tf_op jit(solution)/shard_map/ppermute | solution.py:670
  229.2 4.6 %collective-permute-start.17 = (f32[168,128]{1,0:T(8,128)S(1)}, f32[168,128]{1,0:T(8,128)S(1)}, u32[]{:S(2)}, u32[]{:S(2)}) collective-permute-start(f32[168,128]{1,0:T(8,128)S(1)} %add.253), channel_id=1, source_target_pairs={{0,2},{2,0},{4,6},{6,4},{1,3},{3,1},{5,7},{7,5},{8,10},{10,8},{12,... | collective-permute-start | bytes 258056 | tf_op jit(solution)/shard_map/ppermute | solution.py:670
  229.6 18.6 %collective-permute-start.22 = (f32[608,256]{1,0:T(8,128)S(1)}, f32[608,256]{1,0:T(8,128)S(1)}, u32[]{:S(2)}, u32[]{:S(2)}) collective-permute-start(f32[608,256]{1,0:T(8,128)S(1)} %constant_dynamic-slice_fusion.15), channel_id=1, source_target_pairs={{0,8},{8,0},{16,24},{24,16},{1,9},{9,1},{17,25},{25,17},{2,10},{10... | collective-permute-start | bytes 1867784 | tf_op jit(solution)/shard_map/ppermute | solution.py:670
  233.8 12.0 %collective-permute-start.18 = (f32[168,256]{1,0:T(8,128)S(1)}, f32[168,256]{1,0:T(8,128)S(1)}, u32[]{:S(2)}, u32[]{:S(2)}) collective-permute-start(f32[168,256]{1,0:T(8,128)S(1)} %pad_maximum_fusion.17), channel_id=1, source_target_pairs={{0,16},{8,24},{16,0},{24,8},{1,17},{9,25},{17,1},{25,9},{2,18},{10... | collective-permute-start | bytes 516104 | tf_op jit(solution)/shard_map/ppermute | solution.py:670
  235.9 23.2 %collective-permute-start.52 = (f32[608,256]{1,0:T(8,128)S(1)}, f32[608,256]{1,0:T(8,128)S(1)}, u32[]{:S(2)}, u32[]{:S(2)}) collective-permute-start(f32[608,256]{1,0:T(8,128)S(1)} %constant_dynamic-slice_fusion.3), channel_id=1, source_target_pairs={{0,16},{8,24},{16,0},{24,8},{1,17},{9,25},{17,1},{25,9},{2,18},{10... | collective-permute-start | bytes 1867784 | tf_op jit(solution)/shard_map/ppermute | solution.py:670
  236.3 23.7 %collective-permute-start.42 = (f32[608,256]{1,0:T(8,128)S(1)}, f32[608,256]{1,0:T(8,128)S(1)}, u32[]{:S(2)}, u32[]{:S(2)}) collective-permute-start(f32[608,256]{1,0:T(8,128)S(1)} %constant_dynamic-slice_fusion.7), channel_id=1, source_target_pairs={{0,8},{8,0},{16,24},{24,16},{1,9},{9,1},{17,25},{25,17},{2,10},{10... | collective-permute-start | bytes 1867784 | tf_op jit(solution)/shard_map/ppermute | solution.py:670
  245.9 21.4 %collective-permute-start.19 = (f32[168,512]{1,0:T(8,128)S(1)}, f32[168,512]{1,0:T(8,128)S(1)}, u32[]{:S(2)}, u32[]{:S(2)}) collective-permute-start(f32[168,512]{1,0:T(8,128)S(1)} %pad_maximum_fusion.12), channel_id=1, source_target_pairs={{0,8},{8,0},{16,24},{24,16},{1,9},{9,1},{17,25},{25,17},{2,10},{10... | collective-permute-start | bytes 1032200 | tf_op jit(solution)/shard_map/ppermute | solution.py:670
  246.7 27.3 %collective-permute-start.33 = (f32[304,256]{1,0:T(8,128)S(1)}, f32[304,256]{1,0:T(8,128)S(1)}, u32[]{:S(2)}, u32[]{:S(2)}) collective-permute-start(f32[304,256]{1,0:T(8,128)S(1)} %constant_dynamic-slice_fusion.10), channel_id=1, source_target_pairs={{0,8},{8,0},{16,24},{24,16},{1,9},{9,1},{17,25},{25,17},{2,10},{10... | collective-permute-start | bytes 933896 | tf_op jit(solution)/shard_map/ppermute | solution.py:670
  248.3 26.8 %collective-permute-start.23 = (f32[304,256]{1,0:T(8,128)S(1)}, f32[304,256]{1,0:T(8,128)S(1)}, u32[]{:S(2)}, u32[]{:S(2)}) collective-permute-start(f32[304,256]{1,0:T(8,128)S(1)} %constant_dynamic-slice_fusion.14), channel_id=1, source_target_pairs={{0,16},{8,24},{16,0},{24,8},{1,17},{9,25},{17,1},{25,9},{2,18},{10... | collective-permute-start | bytes 933896 | tf_op jit(solution)/shard_map/ppermute | solution.py:670
  259.3 18.4 %collective-permute-start.53 = (f32[304,256]{1,0:T(8,128)S(1)}, f32[304,256]{1,0:T(8,128)S(1)}, u32[]{:S(2)}, u32[]{:S(2)}) collective-permute-start(f32[304,256]{1,0:T(8,128)S(1)} %constant_dynamic-slice_fusion.2), channel_id=1, source_target_pairs={{0,8},{8,0},{16,24},{24,16},{1,9},{9,1},{17,25},{25,17},{2,10},{10... | collective-permute-start | bytes 933896 | tf_op jit(solution)/shard_map/ppermute | solution.py:670
  260.1 18.4 %collective-permute-start.43 = (f32[304,256]{1,0:T(8,128)S(1)}, f32[304,256]{1,0:T(8,128)S(1)}, u32[]{:S(2)}, u32[]{:S(2)}) collective-permute-start(f32[304,256]{1,0:T(8,128)S(1)} %constant_dynamic-slice_fusion.6), channel_id=1, source_target_pairs={{0,16},{8,24},{16,0},{24,8},{1,17},{9,25},{17,1},{25,9},{2,18},{10... | collective-permute-start | bytes 933896 | tf_op jit(solution)/shard_map/ppermute | solution.py:670
  267.5 56.8 %collective-permute-start.20 = (f32[336,512]{1,0:T(8,128)S(1)}, f32[336,512]{1,0:T(8,128)S(1)}, u32[]{:S(2)}, u32[]{:S(2)}) collective-permute-start(f32[336,512]{1,0:T(8,128)S(1)} %pad_maximum_fusion.5), channel_id=1, source_target_pairs={{0,1},{1,0},{2,3},{3,2},{4,5},{5,4},{6,7},{7,6},{8,9},{9,8},{10,11... | collective-permute-start | bytes 2064392 | tf_op jit(solution)/shard_map/ppermute | solution.py:670
  274.1 8.6 %collective-permute-start.34 = (f32[152,256]{1,0:T(8,128)S(1)}, f32[152,256]{1,0:T(8,128)S(1)}, u32[]{:S(2)}, u32[]{:S(2)}) collective-permute-start(f32[152,256]{1,0:T(8,128)S(1)} %constant_dynamic-slice_fusion.9), channel_id=1, source_target_pairs={{0,2},{2,0},{4,6},{6,4},{1,3},{3,1},{5,7},{7,5},{8,10},{10,8},{12,... | collective-permute-start | bytes 466952 | tf_op jit(solution)/shard_map/ppermute | solution.py:670
  275.2 11.3 %collective-permute-start.24 = (f32[152,256]{1,0:T(8,128)S(1)}, f32[152,256]{1,0:T(8,128)S(1)}, u32[]{:S(2)}, u32[]{:S(2)}) collective-permute-start(f32[152,256]{1,0:T(8,128)S(1)} %constant_dynamic-slice_fusion.13), channel_id=1, source_target_pairs={{0,2},{2,0},{4,6},{6,4},{1,3},{3,1},{5,7},{7,5},{8,10},{10,8},{12,... | collective-permute-start | bytes 466952 | tf_op jit(solution)/shard_map/ppermute | solution.py:670
  277.7 11.5 %collective-permute-start.54 = (f32[152,256]{1,0:T(8,128)S(1)}, f32[152,256]{1,0:T(8,128)S(1)}, u32[]{:S(2)}, u32[]{:S(2)}) collective-permute-start(f32[152,256]{1,0:T(8,128)S(1)} %constant_dynamic-slice_fusion.1), channel_id=1, source_target_pairs={{0,2},{2,0},{4,6},{6,4},{1,3},{3,1},{5,7},{7,5},{8,10},{10,8},{12,... | collective-permute-start | bytes 466952 | tf_op jit(solution)/shard_map/ppermute | solution.py:670
  278.5 13.7 %collective-permute-start.44 = (f32[152,256]{1,0:T(8,128)S(1)}, f32[152,256]{1,0:T(8,128)S(1)}, u32[]{:S(2)}, u32[]{:S(2)}) collective-permute-start(f32[152,256]{1,0:T(8,128)S(1)} %constant_dynamic-slice_fusion.5), channel_id=1, source_target_pairs={{0,2},{2,0},{4,6},{6,4},{1,3},{3,1},{5,7},{7,5},{8,10},{10,8},{12,... | collective-permute-start | bytes 466952 | tf_op jit(solution)/shard_map/ppermute | solution.py:670
  282.7 9.9 %collective-permute-start.35 = (f32[152,128]{1,0:T(8,128)S(1)}, f32[152,128]{1,0:T(8,128)S(1)}, u32[]{:S(2)}, u32[]{:S(2)}) collective-permute-start(f32[152,128]{1,0:T(8,128)S(1)} %constant_dynamic-slice_fusion.8), channel_id=1, source_target_pairs={{0,4},{2,6},{4,0},{6,2},{1,5},{3,7},{5,1},{7,3},{8,12},{10,14},{12... | collective-permute-start | bytes 233480 | tf_op jit(solution)/shard_map/ppermute | solution.py:670
  286.5 13.1 %collective-permute-start.25 = (f32[152,128]{1,0:T(8,128)S(1)}, f32[152,128]{1,0:T(8,128)S(1)}, u32[]{:S(2)}, u32[]{:S(2)}) collective-permute-start(f32[152,128]{1,0:T(8,128)S(1)} %constant_dynamic-slice_fusion.12), channel_id=1, source_target_pairs={{0,4},{2,6},{4,0},{6,2},{1,5},{3,7},{5,1},{7,3},{8,12},{10,14},{12... | collective-permute-start | bytes 233480 | tf_op jit(solution)/shard_map/ppermute | solution.py:670
  289.3 12.0 %collective-permute-start.55 = (f32[152,128]{1,0:T(8,128)S(1)}, f32[152,128]{1,0:T(8,128)S(1)}, u32[]{:S(2)}, u32[]{:S(2)}) collective-permute-start(f32[152,128]{1,0:T(8,128)S(1)} %constant_dynamic-slice_fusion), channel_id=1, source_target_pairs={{0,4},{2,6},{4,0},{6,2},{1,5},{3,7},{5,1},{7,3},{8,12},{10,14},{12... | collective-permute-start | bytes 233480 | tf_op jit(solution)/shard_map/ppermute | solution.py:670
  292.3 11.6 %collective-permute-start.45 = (f32[152,128]{1,0:T(8,128)S(1)}, f32[152,128]{1,0:T(8,128)S(1)}, u32[]{:S(2)}, u32[]{:S(2)}) collective-permute-start(f32[152,128]{1,0:T(8,128)S(1)} %constant_dynamic-slice_fusion.4), channel_id=1, source_target_pairs={{0,4},{2,6},{4,0},{6,2},{1,5},{3,7},{5,1},{7,3},{8,12},{10,14},{12... | collective-permute-start | bytes 233480 | tf_op jit(solution)/shard_map/ppermute | solution.py:670
  292.6 13.7 %collective-permute-start.36 = (f32[152,128]{1,0:T(8,128)S(1)}, f32[152,128]{1,0:T(8,128)S(1)}, u32[]{:S(2)}, u32[]{:S(2)}) collective-permute-start(f32[152,128]{1,0:T(8,128)S(1)} %dynamic-slice_add_fusion.18), channel_id=1, source_target_pairs={{0,4},{2,6},{4,0},{6,2},{1,5},{3,7},{5,1},{7,3},{8,12},{10,14},{12... | collective-permute-start | bytes 233480 | tf_op jit(solution)/shard_map/ppermute | solution.py:670
  299.6 8.2 %collective-permute-start.26 = (f32[152,128]{1,0:T(8,128)S(1)}, f32[152,128]{1,0:T(8,128)S(1)}, u32[]{:S(2)}, u32[]{:S(2)}) collective-permute-start(f32[152,128]{1,0:T(8,128)S(1)} %dynamic-slice_add_fusion.19), channel_id=1, source_target_pairs={{0,4},{2,6},{4,0},{6,2},{1,5},{3,7},{5,1},{7,3},{8,12},{10,14},{12... | collective-permute-start | bytes 233480 | tf_op jit(solution)/shard_map/ppermute | solution.py:670
  301.3 8.2 %collective-permute-start.56 = (f32[152,128]{1,0:T(8,128)S(1)}, f32[152,128]{1,0:T(8,128)S(1)}, u32[]{:S(2)}, u32[]{:S(2)}) collective-permute-start(f32[152,128]{1,0:T(8,128)S(1)} %dynamic-slice_add_fusion.16), channel_id=1, source_target_pairs={{0,4},{2,6},{4,0},{6,2},{1,5},{3,7},{5,1},{7,3},{8,12},{10,14},{12... | collective-permute-start | bytes 233480 | tf_op jit(solution)/shard_map/ppermute | solution.py:670
  303.9 6.9 %collective-permute-start.46 = (f32[152,128]{1,0:T(8,128)S(1)}, f32[152,128]{1,0:T(8,128)S(1)}, u32[]{:S(2)}, u32[]{:S(2)}) collective-permute-start(f32[152,128]{1,0:T(8,128)S(1)} %dynamic-slice_add_fusion.17), channel_id=1, source_target_pairs={{0,4},{2,6},{4,0},{6,2},{1,5},{3,7},{5,1},{7,3},{8,12},{10,14},{12... | collective-permute-start | bytes 233480 | tf_op jit(solution)/shard_map/ppermute | solution.py:670
  306.4 7.6 %collective-permute-start.37 = (f32[152,256]{1,0:T(8,128)S(1)}, f32[152,256]{1,0:T(8,128)S(1)}, u32[]{:S(2)}, u32[]{:S(2)}) collective-permute-start(f32[152,256]{1,0:T(8,128)S(1)} %pad_maximum_fusion.19), channel_id=1, source_target_pairs={{0,2},{2,0},{4,6},{6,4},{1,3},{3,1},{5,7},{7,5},{8,10},{10,8},{12,... | collective-permute-start | bytes 466952 | tf_op jit(solution)/shard_map/ppermute | solution.py:670
  307.9 9.5 %collective-permute-start.27 = (f32[152,256]{1,0:T(8,128)S(1)}, f32[152,256]{1,0:T(8,128)S(1)}, u32[]{:S(2)}, u32[]{:S(2)}) collective-permute-start(f32[152,256]{1,0:T(8,128)S(1)} %pad_maximum_fusion.18), channel_id=1, source_target_pairs={{0,2},{2,0},{4,6},{6,4},{1,3},{3,1},{5,7},{7,5},{8,10},{10,8},{12,... | collective-permute-start | bytes 466952 | tf_op jit(solution)/shard_map/ppermute | solution.py:670
  309.5 10.6 %collective-permute-start.57 = (f32[152,256]{1,0:T(8,128)S(1)}, f32[152,256]{1,0:T(8,128)S(1)}, u32[]{:S(2)}, u32[]{:S(2)}) collective-permute-start(f32[152,256]{1,0:T(8,128)S(1)} %pad_maximum_fusion.21), channel_id=1, source_target_pairs={{0,2},{2,0},{4,6},{6,4},{1,3},{3,1},{5,7},{7,5},{8,10},{10,8},{12,... | collective-permute-start | bytes 466952 | tf_op jit(solution)/shard_map/ppermute | solution.py:670
  310.8 10.7 %collective-permute-start.47 = (f32[152,256]{1,0:T(8,128)S(1)}, f32[152,256]{1,0:T(8,128)S(1)}, u32[]{:S(2)}, u32[]{:S(2)}) collective-permute-start(f32[152,256]{1,0:T(8,128)S(1)} %pad_maximum_fusion.20), channel_id=1, source_target_pairs={{0,2},{2,0},{4,6},{6,4},{1,3},{3,1},{5,7},{7,5},{8,10},{10,8},{12,... | collective-permute-start | bytes 466952 | tf_op jit(solution)/shard_map/ppermute | solution.py:670
  314.8 13.9 %collective-permute-start.38 = (f32[304,256]{1,0:T(8,128)}, f32[304,256]{1,0:T(8,128)S(1)}, u32[]{:S(2)}, u32[]{:S(2)}) collective-permute-start(f32[304,256]{1,0:T(8,128)} %pad_maximum_fusion.14), channel_id=1, source_target_pairs={{0,8},{8,0},{16,24},{24,16},{1,9},{9,1},{17,25},{25,17},{2,10},{10... | collective-permute-start | bytes 933896 | tf_op jit(solution)/shard_map/ppermute | solution.py:670
  318.1 10.8 %collective-permute-start.28 = (f32[304,256]{1,0:T(8,128)}, f32[304,256]{1,0:T(8,128)}, u32[]{:S(2)}, u32[]{:S(2)}) collective-permute-start(f32[304,256]{1,0:T(8,128)} %pad_maximum_fusion.13), channel_id=1, source_target_pairs={{0,16},{8,24},{16,0},{24,8},{1,17},{9,25},{17,1},{25,9},{2,18},{10... | collective-permute-start | bytes 933896 | tf_op jit(solution)/shard_map/ppermute | solution.py:670
  320.9 10.6 %collective-permute-start.58 = (f32[304,256]{1,0:T(8,128)}, f32[304,256]{1,0:T(8,128)}, u32[]{:S(2)}, u32[]{:S(2)}) collective-permute-start(f32[304,256]{1,0:T(8,128)} %pad_maximum_fusion.16), channel_id=1, source_target_pairs={{0,8},{8,0},{16,24},{24,16},{1,9},{9,1},{17,25},{25,17},{2,10},{10... | collective-permute-start | bytes 933896 | tf_op jit(solution)/shard_map/ppermute | solution.py:670
  322.3 12.1 %collective-permute-start.48 = (f32[304,256]{1,0:T(8,128)}, f32[304,256]{1,0:T(8,128)}, u32[]{:S(2)}, u32[]{:S(2)}) collective-permute-start(f32[304,256]{1,0:T(8,128)} %pad_maximum_fusion.15), channel_id=1, source_target_pairs={{0,16},{8,24},{16,0},{24,8},{1,17},{9,25},{17,1},{25,9},{2,18},{10... | collective-permute-start | bytes 933896 | tf_op jit(solution)/shard_map/ppermute | solution.py:670
  328.8 18.7 %collective-permute-start.39 = (f32[608,256]{1,0:T(8,128)S(1)}, f32[608,256]{1,0:T(8,128)S(1)}, u32[]{:S(2)}, u32[]{:S(2)}) collective-permute-start(f32[608,256]{1,0:T(8,128)S(1)} %pad_maximum_fusion.7), channel_id=1, source_target_pairs={{0,16},{8,24},{16,0},{24,8},{1,17},{9,25},{17,1},{25,9},{2,18},{10... | collective-permute-start | bytes 1867784 | tf_op jit(solution)/shard_map/ppermute | solution.py:670
  330.0 17.8 %collective-permute-start.29 = (f32[608,256]{1,0:T(8,128)S(1)}, f32[608,256]{1,0:T(8,128)S(1)}, u32[]{:S(2)}, u32[]{:S(2)}) collective-permute-start(f32[608,256]{1,0:T(8,128)S(1)} %pad_maximum_fusion.6), channel_id=1, source_target_pairs={{0,8},{8,0},{16,24},{24,16},{1,9},{9,1},{17,25},{25,17},{2,10},{10... | collective-permute-start | bytes 1867784 | tf_op jit(solution)/shard_map/ppermute | solution.py:670
  332.6 26.0 %collective-permute-start.59 = (f32[608,256]{1,0:T(8,128)S(1)}, f32[608,256]{1,0:T(8,128)S(1)}, u32[]{:S(2)}, u32[]{:S(2)}) collective-permute-start(f32[608,256]{1,0:T(8,128)S(1)} %pad_maximum_fusion.9), channel_id=1, source_target_pairs={{0,16},{8,24},{16,0},{24,8},{1,17},{9,25},{17,1},{25,9},{2,18},{10... | collective-permute-start | bytes 1867784 | tf_op jit(solution)/shard_map/ppermute | solution.py:670
  335.4 23.4 %collective-permute-start.49 = (f32[608,256]{1,0:T(8,128)S(1)}, f32[608,256]{1,0:T(8,128)S(1)}, u32[]{:S(2)}, u32[]{:S(2)}) collective-permute-start(f32[608,256]{1,0:T(8,128)S(1)} %pad_maximum_fusion.8), channel_id=1, source_target_pairs={{0,8},{8,0},{16,24},{24,16},{1,9},{9,1},{17,25},{25,17},{2,10},{10... | collective-permute-start | bytes 1867784 | tf_op jit(solution)/shard_map/ppermute | solution.py:670
  347.7 11.9 %collective-permute-start.40 = (f32[1216,256]{1,0:T(8,128)S(1)}, f32[1216,256]{1,0:T(8,128)S(1)}, u32[]{:S(2)}, u32[]{:S(2)}) collective-permute-start(f32[1216,256]{1,0:T(8,128)S(1)} %pad_maximum_fusion.2), channel_id=1, source_target_pairs={{0,1},{1,0},{2,3},{3,2},{4,5},{5,4},{6,7},{7,6},{8,9},{9,8},{10,11... | collective-permute-start | bytes 3735560 | tf_op jit(solution)/shard_map/ppermute | solution.py:670
  348.0 11.8 %collective-permute-start.30 = (f32[1216,256]{1,0:T(8,128)S(1)}, f32[1216,256]{1,0:T(8,128)S(1)}, u32[]{:S(2)}, u32[]{:S(2)}) collective-permute-start(f32[1216,256]{1,0:T(8,128)S(1)} %pad_maximum_fusion.1), channel_id=1, source_target_pairs={{0,1},{1,0},{2,3},{3,2},{4,5},{5,4},{6,7},{7,6},{8,9},{9,8},{10,11... | collective-permute-start | bytes 3735560 | tf_op jit(solution)/shard_map/ppermute | solution.py:670
  358.8 3.0 collective-permute-start.60
  359.0 4.5 %collective-permute-start.50 = (f32[1216,256]{1,0:T(8,128)S(1)}, f32[1216,256]{1,0:T(8,128)S(1)}, u32[]{:S(2)}, u32[]{:S(2)}) collective-permute-start(f32[1216,256]{1,0:T(8,128)S(1)} %pad_maximum_fusion.3), channel_id=1, source_target_pairs={{0,1},{1,0},{2,3},{3,2},{4,5},{5,4},{6,7},{7,6},{8,9},{9,8},{10,11... | collective-permute-start | bytes 3735560 | tf_op jit(solution)/shard_map/ppermute | solution.py:670
  (64 other events, 493.0 us)
